TPU v7x, 32 devices: a whole 2x2x4 slice. The times are simulated.
32 devices in a mesh: grp: 4 (over x, core), seq: 8 (over z, y).
Axes of the slice: x: 2, y: 2, z: 4, core: 2. Of those that a mesh axis runs over, the one named last changes fastest.
Arguments:
- tokens: bfloat16 [4096, 2048], P(('grp', 'seq')), may hold values from -6 to 6
- doc_lengths: int32 [4, 8], P('grp'), may hold values from 1 to 897, 1024 in all within a row
- cotangent: bfloat16 [4096, 2048], P(('grp', 'seq')), may hold values from -6 to 6
- attn_gain: bfloat16 [2048], P(('grp', 'seq')), may hold values from 0.5 to 1.5
- query_weight: bfloat16 [2048, 1024], P(('grp', 'seq')), may hold values from -0.125 to 0.125
- key_weight: bfloat16 [2048, 1024], P(('grp', 'seq')), may hold values from -0.125 to 0.125
- value_weight: bfloat16 [2048, 2048], P(('grp', 'seq')), may hold values from -0.125 to 0.125
- gate_weight: bfloat16 [2048, 2048], P(('grp', 'seq')), may hold values from -0.125 to 0.125
- rank_in: bfloat16 [2048, 16], P(('grp', 'seq')), may hold values from -0.125 to 0.125
- rank_out: bfloat16 [1024, 16], P(('grp', 'seq')), may hold values from -3 to 3
- decay_bias: bfloat16 [1024], P(('grp', 'seq')), may hold values from -1 to 12, as said below
- head_gain: bfloat16 [512], P(('grp', 'seq')), may hold values from 0.5 to 1.5
- out_weight: bfloat16 [2048, 2048], P(('grp', 'seq')), may hold values from -0.25 to 0.25
- mlp_gain: bfloat16 [2048], P(('grp', 'seq')), may hold values from 0.5 to 1.5
- mlp_gate_weight: bfloat16 [2048, 5632], P(('grp', 'seq')), may hold values from -0.125 to 0.125
- mlp_up_weight: bfloat16 [2048, 5632], P(('grp', 'seq')), may hold values from -0.125 to 0.125
- down_weight: bfloat16 [2048, 5632], P(('grp', 'seq')), may hold values from -0.109375 to 0.109375
Outputs:
- layer_out: float32 [4096, 2048], P(('grp', 'seq'))
- tokens_grad: float32 [4096, 2048], P(('grp', 'seq'))
- attn_gain_grad: float32 [2048], P(('grp', 'seq'))
- query_grad: float32 [2048, 1024], P(('grp', 'seq'))
- key_grad: float32 [2048, 1024], P(('grp', 'seq'))
- value_grad: float32 [2048, 2048], P(('grp', 'seq'))
- gate_grad: float32 [2048, 2048], P(('grp', 'seq'))
- rank_in_grad: float32 [2048, 16], P(('grp', 'seq'))
- rank_out_grad: float32 [1024, 16], P(('grp', 'seq'))
- decay_bias_grad: float32 [1024], P(('grp', 'seq'))
- head_gain_grad: float32 [512], P(('grp', 'seq'))
- out_weight_grad: float32 [2048, 2048], P(('grp', 'seq'))
- mlp_gain_grad: float32 [2048], P(('grp', 'seq'))
- mlp_gate_grad: float32 [2048, 5632], P(('grp', 'seq'))
- mlp_up_grad: float32 [2048, 5632], P(('grp', 'seq'))
- down_grad: float32 [2048, 5632], P(('grp', 'seq'))
Inputs may be any that keep to these rules, and one draw needn't show every extreme that they name: `doc_lengths`: row s lists the lengths of the 8 documents packed, in order, into sequence s; they sum to 1024, and one of them is 897. `decay_bias`: one bias a key channel.
All inputs are finite; a program needn't handle non-finite values.
Results may differ from a plain program's by a relative error of at most 0.035.
Values may be sent and summed in bfloat16 or wider, within the bound.
A program may use at most 576 MiB of HBM per device.

v0:
```python
import jax
import jax.numpy as jnp
from jax import lax
from jax.sharding import PartitionSpec as P

H = 4
DK = 256
DV = 512
FF = 5632
CH = 64


HIGHEST = lax.Precision.HIGHEST
norm_eps = 1e-06
head_eps = 0.25
decay_norm = 16.0


def prefix(value, axis, combine, identity, reverse):
    peers, index = (lax.axis_size(axis), lax.axis_index(axis))
    everything = jax.tree.map(lambda part: lax.all_gather(part, axis), value)
    start = jax.tree.map(
        lambda part, zero: jnp.broadcast_to(jnp.asarray(zero, part.dtype), part.shape),
        value,
        identity,
    )

    def lap(k, before):
        at = peers - 1 - k if reverse else k
        reached = at > index if reverse else at < index
        new = combine(before, jax.tree.map(lambda part: part[at], everything))
        return jax.tree.map(lambda a, b: jnp.where(reached, a, b), new, before)

    return lax.fori_loop(0, peers, lap, start)


def rms_scale(row_values):
    return row_values * lax.rsqrt(
        jnp.mean(row_values * row_values, axis=-1, keepdims=True) + norm_eps
    )


def head_gate(mixed_rows, out_gate, head_scale):
    normed = (
        mixed_rows
        * lax.rsqrt(jnp.mean(mixed_rows * mixed_rows, axis=-1, keepdims=True) + head_eps)
        * head_scale
    )
    return (normed * jax.nn.silu(out_gate.reshape(mixed_rows.shape))).reshape(out_gate.shape)


def dot_plain(left, right):
    return jnp.dot(left, right, preferred_element_type=jnp.float32)


def dot_rows(left, right):
    return lax.dot_general(
        left, right, (((1,), (1,)), ((), ())), preferred_element_type=jnp.float32
    )


def dot_cols(left, right):
    return lax.dot_general(
        left, right, (((0,), (0,)), ((), ())), preferred_element_type=jnp.float32
    )


def block_step(carried, inputs):
    state_rows, segment_before = carried
    query_block, key_block, value_block, decay_block, segment_block = inputs
    positions = lax.iota(jnp.int32, query_block.shape[0])
    cumulative = jnp.cumsum(decay_block, axis=0)
    final_sum = cumulative[-1]
    query_scaled = query_block * query_block.shape[-1] ** (-0.5)
    query_decay = query_scaled * jnp.exp(cumulative)
    key_end = key_block * jnp.exp(final_sum[None] - cumulative)
    allowed_bool = (positions[:, None] >= positions[None, :]) & (
        segment_block[:, None] == segment_block[None, :]
    )
    allowed = allowed_bool.astype(query_block.dtype)
    spread = cumulative[:, None] - cumulative[None, :]
    inside = allowed_bool[:, :, None, None]
    relative = jnp.where(inside, jnp.exp(jnp.where(inside, spread, 0.0)), 0.0)
    scores = (
        jnp.einsum("thc,shc,tshc->hts", query_scaled, key_block, relative, precision=HIGHEST)
        * allowed[None]
    )
    outputs = jnp.einsum("hts,shv->thv", scores, value_block, precision=HIGHEST)
    entry_rows = (segment_block == segment_before).astype(query_block.dtype)
    outputs = outputs + entry_rows[:, None, None] * jnp.einsum(
        "thc,hcv->thv", query_decay, state_rows, precision=HIGHEST
    )
    seg_last = segment_block[-1]
    tail_mask = (segment_block == seg_last).astype(query_block.dtype)
    passes = (seg_last == segment_before).astype(query_block.dtype)
    state_rows = passes * jnp.exp(final_sum)[:, :, None] * state_rows + jnp.einsum(
        "shc,shv->hcv", key_end * tail_mask[:, None, None], value_block, precision=HIGHEST
    )
    return ((state_rows, seg_last), outputs)


def mixer_local(query_heads, key_heads, value_heads, decay_heads, segments, segment_before):
    row_count = query_heads.shape[0]
    blocks = row_count // CH

    def to_blocks(array_rows):
        return array_rows.reshape((blocks, CH) + array_rows.shape[1:])

    initial = (jnp.zeros((H, DK, DV), jnp.float32), segment_before)
    final_carry, outputs = lax.scan(
        jax.checkpoint(block_step),
        initial,
        (
            to_blocks(query_heads),
            to_blocks(key_heads),
            to_blocks(value_heads),
            to_blocks(decay_heads),
            to_blocks(segments),
        ),
    )
    return (
        outputs.reshape(row_count, H, DV),
        final_carry[0],
        jnp.exp(jnp.sum(decay_heads, axis=0)),
    )


def lift_rows(query_heads, decay_heads, entry_mask):
    return (
        query_heads
        * query_heads.shape[-1] ** (-0.5)
        * jnp.exp(jnp.cumsum(decay_heads, axis=0))
        * entry_mask[:, None, None]
    )


def carry_join(earlier, later):
    keep_early, decay_early, state_early = earlier
    keep_late, decay_late, state_late = later
    return (
        keep_early * keep_late,
        decay_early * decay_late,
        keep_late * decay_late[:, :, None] * state_early + state_late,
    )


def return_join(earlier, later):
    keep_high, decay_high, grad_high = earlier
    keep_low, decay_low, grad_low = later
    return (
        keep_high * keep_low,
        decay_high * decay_low,
        grad_low + keep_low * decay_low[:, :, None] * grad_high,
    )


def local(
    tokens,
    doc_lengths,
    cotangent,
    attn_gain,
    query_weight,
    key_weight,
    value_weight,
    gate_weight,
    rank_in,
    rank_out,
    decay_bias,
    head_gain,
    out_weight,
    mlp_gain,
    mlp_gate_weight,
    mlp_up_weight,
    down_weight,
):
    row_count = tokens.shape[0]
    key_total = H * DK
    value_total = H * DV
    token_rows = tokens.astype(jnp.float32)
    rhat_in, norm_in_back = jax.vjp(rms_scale, token_rows)
    start_row = lax.axis_index("seq") * row_count
    positions = start_row + lax.iota(jnp.int32, row_count)
    doc_ends = jnp.cumsum(doc_lengths[0])
    segments = jnp.sum((doc_ends[None, :] <= positions[:, None]).astype(jnp.int32), axis=1)
    prior_seg = jnp.sum((doc_ends <= start_row - 1).astype(jnp.int32))
    segment_before = jnp.where(start_row == 0, -1, prior_seg)
    entry_mask = (segments == segment_before).astype(jnp.float32)
    passes = (segments[-1] == segment_before).astype(jnp.float32).reshape(1, 1, 1)
    gain_piece = lax.all_gather(attn_gain, ("grp", "seq"), axis=0, tiled=True)
    query_piece = lax.all_gather(query_weight, ("grp", "seq"), axis=0, tiled=True)
    key_piece = lax.all_gather(key_weight, ("grp", "seq"), axis=0, tiled=True)
    value_piece = lax.all_gather(value_weight, ("grp", "seq"), axis=0, tiled=True)
    gate_piece = lax.all_gather(gate_weight, ("grp", "seq"), axis=0, tiled=True)
    rank_piece = lax.all_gather(rank_in, ("grp", "seq"), axis=0, tiled=True)
    low_piece = lax.all_gather(rank_out, ("grp", "seq"), axis=0, tiled=True)
    bias_piece = lax.all_gather(decay_bias, ("grp", "seq"), axis=0, tiled=True)
    head_piece = lax.all_gather(head_gain, ("grp", "seq"), axis=0, tiled=True)
    normed = (rhat_in * gain_piece.astype(jnp.float32)).astype(jnp.bfloat16)
    total_query = dot_plain(normed, query_piece)
    total_key = dot_plain(normed, key_piece)
    total_value = dot_plain(normed, value_piece)
    out_gate = dot_plain(normed, gate_piece)
    total_rank = dot_plain(normed, rank_piece)
    normed_in = normed
    query_low = total_query.astype(jnp.bfloat16)
    key_low = total_key.astype(jnp.bfloat16)
    value_low = total_value.astype(jnp.bfloat16)
    rank_low = total_rank.astype(jnp.bfloat16)
    decay_logit = dot_rows(rank_low, low_piece) + bias_piece.astype(jnp.float32)

    def decay_of(logit_rows):
        return jax.nn.log_sigmoid(logit_rows) / decay_norm

    log_decay, decay_back = jax.vjp(decay_of, decay_logit)
    query_heads = query_low.astype(jnp.float32).reshape(row_count, H, DK)
    key_heads = key_low.astype(jnp.float32).reshape(row_count, H, DK)
    value_heads = value_low.astype(jnp.float32).reshape(row_count, H, DV)
    decay_heads = log_decay.reshape(row_count, H, DK)

    def core_part(query_rows, key_rows, value_rows, decay_rows):
        return mixer_local(query_rows, key_rows, value_rows, decay_rows, segments, segment_before)

    core_out, core_back = jax.vjp(core_part, query_heads, key_heads, value_heads, decay_heads)
    local_mix, local_end, local_decay = core_out
    identity = (
        jnp.ones((1, 1, 1), jnp.float32),
        jnp.ones((H, DK), jnp.float32),
        jnp.zeros((H, DK, DV), jnp.float32),
    )
    state_in = prefix((passes, local_decay, local_end), "seq", carry_join, identity, False)[2]

    def entry_part(query_rows, decay_rows):
        return jnp.einsum(
            "thc,hcv->thv",
            lift_rows(query_rows, decay_rows, entry_mask),
            state_in,
            precision=HIGHEST,
        )

    entry_mix, entry_back = jax.vjp(entry_part, query_heads, decay_heads)
    mixed_rows = local_mix + entry_mix
    gated_f, head_back = jax.vjp(head_gate, mixed_rows, out_gate, head_piece.astype(jnp.float32))
    gated_rows = gated_f.astype(jnp.bfloat16)
    residual = token_rows + dot_rows(
        gated_rows, lax.all_gather(out_weight, ("grp", "seq"), axis=0, tiled=True)
    )
    rhat_mid, norm_mid_back = jax.vjp(rms_scale, residual)
    gain_piece = lax.all_gather(mlp_gain, ("grp", "seq"), axis=0, tiled=True)
    gate_piece = lax.all_gather(mlp_gate_weight, ("grp", "seq"), axis=0, tiled=True)
    up_piece = lax.all_gather(mlp_up_weight, ("grp", "seq"), axis=0, tiled=True)
    normed = (rhat_mid * gain_piece.astype(jnp.float32)).astype(jnp.bfloat16)
    gate_pre = dot_plain(normed, gate_piece)
    up_pre = dot_plain(normed, up_piece)
    sig_gate = jax.nn.sigmoid(gate_pre)
    silu_gate = gate_pre * sig_gate
    hidden = (silu_gate * up_pre).astype(jnp.bfloat16)
    layer_out = residual + dot_rows(
        hidden, lax.all_gather(down_weight, ("grp", "seq"), axis=0, tiled=True)
    )
    grad_hidden = dot_plain(
        cotangent, lax.all_gather(down_weight, ("grp", "seq"), axis=0, tiled=True)
    )
    grad_gate = (grad_hidden * up_pre * sig_gate * (1.0 + gate_pre * (1.0 - sig_gate))).astype(
        jnp.bfloat16
    )
    grad_up = (grad_hidden * silu_gate).astype(jnp.bfloat16)
    gain_piece = lax.all_gather(mlp_gain, ("grp", "seq"), axis=0, tiled=True)
    gate_piece = lax.all_gather(mlp_gate_weight, ("grp", "seq"), axis=0, tiled=True)
    up_piece = lax.all_gather(mlp_up_weight, ("grp", "seq"), axis=0, tiled=True)
    columns = dot_rows(grad_gate, gate_piece) + dot_rows(grad_up, up_piece)
    rhat_cols = rhat_mid
    grad_rows = columns * gain_piece.astype(jnp.float32)
    gain_grad = jnp.sum(columns * rhat_cols, axis=0)
    grad_rhat_mid = grad_rows
    mlp_gain_part = gain_grad
    grad_residual = cotangent.astype(jnp.float32) + norm_mid_back(grad_rhat_mid)[0]
    normed_cols = normed
    mlp_rows = lax.psum_scatter(
        jnp.concatenate(
            [
                dot_cols(normed_cols, grad_gate),
                dot_cols(normed_cols, grad_up),
                dot_cols(cotangent, hidden),
            ],
            axis=1,
        ),
        ("grp", "seq"),
        scatter_dimension=0,
        tiled=True,
    )
    grad_branch = grad_residual.astype(jnp.bfloat16)
    grad_gated = dot_plain(
        grad_branch, lax.all_gather(out_weight, ("grp", "seq"), axis=0, tiled=True)
    )
    grad_mixed, grad_gate_f, head_gain_part = head_back(grad_gated)
    grad_out_gate = grad_gate_f.astype(jnp.bfloat16)
    lifted = lift_rows(query_heads, decay_heads, entry_mask)
    direct = jnp.einsum("thc,thv->hcv", lifted, grad_mixed, precision=HIGHEST)
    state_grad = prefix((passes, local_decay, direct), "seq", return_join, identity, True)[2]
    decay_grad = passes[0] * jnp.sum(state_grad * state_in, axis=2)
    entry_query, entry_decay = entry_back(grad_mixed)
    core_query, core_key, core_value, core_decay = core_back((grad_mixed, state_grad, decay_grad))
    grad_query = (entry_query + core_query).reshape(row_count, key_total).astype(jnp.bfloat16)
    grad_key = core_key.reshape(row_count, key_total).astype(jnp.bfloat16)
    grad_value = core_value.reshape(row_count, value_total).astype(jnp.bfloat16)
    grad_logit = decay_back((entry_decay + core_decay).reshape(row_count, key_total))[0].astype(
        jnp.bfloat16
    )
    bias_part = jnp.sum(grad_logit.astype(jnp.float32), axis=0)
    rank_out_part = dot_cols(grad_logit, rank_low)
    grad_rank = dot_plain(grad_logit, low_piece).astype(jnp.bfloat16)
    rank_in_part = dot_cols(normed_in, grad_rank)
    gain_piece = lax.all_gather(attn_gain, ("grp", "seq"), axis=0, tiled=True)
    query_piece = lax.all_gather(query_weight, ("grp", "seq"), axis=0, tiled=True)
    key_piece = lax.all_gather(key_weight, ("grp", "seq"), axis=0, tiled=True)
    value_piece = lax.all_gather(value_weight, ("grp", "seq"), axis=0, tiled=True)
    gate_piece = lax.all_gather(gate_weight, ("grp", "seq"), axis=0, tiled=True)
    rank_piece = lax.all_gather(rank_in, ("grp", "seq"), axis=0, tiled=True)
    columns = (
        dot_rows(grad_query, query_piece)
        + dot_rows(grad_key, key_piece)
        + dot_rows(grad_value, value_piece)
        + dot_rows(grad_out_gate, gate_piece)
        + dot_rows(grad_rank, rank_piece)
    )
    rhat_cols = rhat_in
    grad_rows = columns * gain_piece.astype(jnp.float32)
    gain_grad = jnp.sum(columns * rhat_cols, axis=0)
    tokens_grad = grad_residual + norm_in_back(grad_rows)[0]
    normed_cols = normed_in
    attn_rows = lax.psum_scatter(
        jnp.concatenate(
            [
                dot_cols(normed_cols, grad_query),
                dot_cols(normed_cols, grad_key),
                dot_cols(normed_cols, grad_value),
                dot_cols(normed_cols, grad_out_gate),
                dot_cols(grad_branch, gated_rows),
            ],
            axis=1,
        ),
        ("grp", "seq"),
        scatter_dimension=0,
        tiled=True,
    )
    small_sums = (
        lax.psum_scatter(gain_grad, ("grp", "seq"), scatter_dimension=0, tiled=True),
        lax.psum_scatter(mlp_gain_part, ("grp", "seq"), scatter_dimension=0, tiled=True),
        lax.psum_scatter(head_gain_part, ("grp", "seq"), scatter_dimension=0, tiled=True),
        lax.psum_scatter(bias_part, ("grp", "seq"), scatter_dimension=0, tiled=True),
        lax.psum_scatter(rank_in_part, ("grp", "seq"), scatter_dimension=0, tiled=True),
        lax.psum_scatter(rank_out_part, ("grp", "seq"), scatter_dimension=0, tiled=True),
    )
    query_grad = attn_rows[:, :key_total]
    key_grad = attn_rows[:, key_total : 2 * key_total]
    value_grad = attn_rows[:, 2 * key_total : 2 * key_total + value_total]
    gate_grad = attn_rows[:, 2 * key_total + value_total : 2 * key_total + 2 * value_total]
    out_weight_grad = attn_rows[:, 2 * key_total + 2 * value_total :]
    mlp_gate_grad = mlp_rows[:, :FF]
    mlp_up_grad = mlp_rows[:, FF : 2 * FF]
    down_grad = mlp_rows[:, 2 * FF :]
    return (
        layer_out,
        tokens_grad,
        small_sums[0],
        query_grad,
        key_grad,
        value_grad,
        gate_grad,
        small_sums[4],
        small_sums[5],
        small_sums[3],
        small_sums[2],
        out_weight_grad,
        small_sums[1],
        mlp_gate_grad,
        mlp_up_grad,
        down_grad,
    )


def solution(mesh):
    placed = (
        P(("grp", "seq"), None),
        P("grp", None),
        P(("grp", "seq"), None),
        P(("grp", "seq")),
        P(("grp", "seq"), None),
        P(("grp", "seq"), None),
        P(("grp", "seq"), None),
        P(("grp", "seq"), None),
        P(("grp", "seq"), None),
        P(("grp", "seq"), None),
        P(("grp", "seq")),
        P(("grp", "seq")),
        P(("grp", "seq"), None),
        P(("grp", "seq")),
        P(("grp", "seq"), None),
        P(("grp", "seq"), None),
        P(("grp", "seq"), None),
    )
    return jax.shard_map(
        local,
        mesh=mesh,
        in_specs=placed,
        out_specs=(
            P(("grp", "seq"), None),
            P(("grp", "seq"), None),
            P(("grp", "seq")),
            P(("grp", "seq"), None),
            P(("grp", "seq"), None),
            P(("grp", "seq"), None),
            P(("grp", "seq"), None),
            P(("grp", "seq"), None),
            P(("grp", "seq"), None),
            P(("grp", "seq")),
            P(("grp", "seq")),
            P(("grp", "seq"), None),
            P(("grp", "seq")),
            P(("grp", "seq"), None),
            P(("grp", "seq"), None),
            P(("grp", "seq"), None),
        ),
        check_vma=False,
    )
```

profile of v0, /device:TPU:9, one launch (start us, length us, event | category | flops | bytes accessed | tf_op | source)
XLA Modules:
  0.0 5198.5 jit_solution(15688301153293905398)
XLA Ops:
  15.8 40.4 all-reduce.12
  56.1 59.6 %all-gather.2 = bf16[32,64,16]{1,2,0:T(8,128)(2,1)S(1)} all-gather(bf16[1,64,16]{1,2,0:T(8,128)(2,1)} %bitcast.477), channel_id=1, replica_groups=mesh['grp'=4,'seq'=8] {'grp','seq'}, dimensions={0}, use_global_device_ids=true | all-gather | bytes 67584 | tf_op jit(solution)/shard_map/all_gather | solution.py:194
  115.9 62.8 %all-gather.3 = bf16[32,32,16]{1,2,0:T(8,128)(2,1)S(1)} all-gather(bf16[1,32,16]{1,2,0:T(8,128)(2,1)} %bitcast.478), channel_id=1, replica_groups=mesh['grp'=4,'seq'=8] {'grp','seq'}, dimensions={0}, use_global_device_ids=true | all-gather | bytes 33792 | tf_op jit(solution)/shard_map/all_gather | solution.py:195
  195.9 22.1 all-gather.17.cloned.1.call-done
  229.1 97.0 %while.74 = (s32[]{:T(128)}, f32[4,256,512]{2,1,0:T(8,128)S(1)}, s32[]{:T(128)}, f32[2,64,4,512]{3,1,0,2:T(8,128)}, f32[2,4,256,512]{3,2,1,0:T(8,128)}, /*index=...) while((s32[]{:T(128)}, f32[4,256,512]{2,1,0:T(8,128)S(1)}, ...), condition=%wide.region_6.7_spmd.clone, body=%wide.region_4.6_spmd.clone.sunk | while | flops 938558720 | bytes 52251108 | solution.py:110
  350.0 24.8 all_gather.83
  379.3 172.2 %all-gather.31.cloned.1.call-done = f32[32,256,512]{2,1,0:T(8,128)} async-done(((f32[4,256,512]{2,1,0:T(8,128)}), f32[32,256,512]{2,1,0:T(8,128)}) %all-gather.31.cloned.1.call-update) | async-done | bytes 16777232 | tf_op jit(solution)/shard_map/all_gather | solution.py:21
  551.6 27.6 while.75
  585.9 46.8 all-gather.21.cloned.1.call-done
  640.7 70.8 %all-gather.23.cloned.1.call-done = bf16[2048,2048]{1,0:T(8,128)(2,1)} async-done(((bf16[64,2048]{1,0:T(8,128)(2,1)}), bf16[2048,2048]{1,0:T(8,128)(2,1)}) %all-gather.23.cloned.1.call-update) | async-done | bytes 8388624 | tf_op jit(solution)/shard_map/all_gather | solution.py:245
  718.1 137.8 %all-gather.25.cloned.1.call-done = bf16[2048,5632]{1,0:T(8,128)(2,1)} async-done(((bf16[64,5632]{1,0:T(8,128)(2,1)}), bf16[2048,5632]{1,0:T(8,128)(2,1)}) %all-gather.25.cloned.1.call-update) | async-done | bytes 23068688 | tf_op jit(solution)/shard_map/all_gather | solution.py:249
  868.5 133.2 %all-gather.27.cloned.1.call-done = bf16[2048,5632]{1,0:T(8,128)(2,1)} async-done(((bf16[64,5632]{1,0:T(8,128)(2,1)}), bf16[2048,5632]{1,0:T(8,128)(2,1)}) %all-gather.27.cloned.1.call-update) | async-done | bytes 23068688 | tf_op jit(solution)/shard_map/all_gather | solution.py:250
  1014.0 133.4 %all-gather.29.cloned.1.call-done = bf16[2048,5632]{1,0:T(8,128)(2,1)} async-done(((bf16[64,5632]{1,0:T(8,128)(2,1)}), bf16[2048,5632]{1,0:T(8,128)(2,1)}) %all-gather.29.cloned.1.call-update) | async-done | bytes 23068688 | tf_op jit(solution)/shard_map/all_gather | solution.py:258
  1204.3 21.5 fusion.154
  1225.9 18.3 fusion.153
  1244.1 18.0 convolution_bitcast_fusion.2
  1262.1 165.8 %all-gather.33.cloned.1.call-done = f32[32,256,512]{2,1,0:T(8,128)} async-done(((f32[4,256,512]{2,1,0:T(8,128)}), f32[32,256,512]{2,1,0:T(8,128)}) %all-gather.33.cloned.1.call-update) | async-done | bytes 16777232 | tf_op jit(solution)/shard_map/all_gather | solution.py:21
  1428.0 27.6 while.76
  1461.3 97.8 %while.73 = (s32[]{:T(128)}, f32[4,256,512]{2,1,0:T(8,128)S(1)}, f32[2,64,4,256]{3,1,0,2:T(8,128)}, bf16[2,64,4,256]{3,1,2,0:T(8,128)(2,1)}, bf16[2,64,4,512]{3,...) while((s32[]{:T(128)}, f32[4,256,512]{2,1,0:T(8,128)S(1)}, ...), condition=%wide.region_24.25_spmd, body=%wide.region_17.24_spmd.sunk | while | flops 1937606912 | bytes 83680984 | solution.py:110
  1578.6 88.6 %pad_maximum_fusion = f32[2048,16896]{1,0:T(8,128)} fusion(f32[2048,5632]{1,0:T(8,128)} %convolution_bitcast_fusion.2, f32[2048,5632]{1,0:T(8,128)} %fusion.154, f32[2048,5632]{1,0:T(8,128)} %fusion.153), kind=kLoop, calls=%fused_computation.134 | loop fusion | flops 69206016 | bytes 276824064 | tf_op jit(solution)/shard_map/concatenate | solution.py:279
  1704.1 61.5 %copy.234 = f32[2048,8192]{1,0:T(8,128)} copy(f32[2048,8192]{0,1:T(8,128)} %convolution_dynamic-update-slice_fusion) | data formatting | bytes 134217728
  1798.5 41.1 all-reduce.11
  1846.0 1934.9 %all-reduce.15.cloned.1.call-done = f32[2048,16896]{1,0:T(8,128)} async-done(((f32[2048,16896]{1,0:T(8,128)}), f32[2048,16896]{1,0:T(8,128)}) %all-reduce.15.cloned.1.call-update) | async-done | bytes 138412048
  3786.1 1401.1 %reduce-scatter.10.cloned.1.call-done = f32[64,8192]{1,0:T(8,128)} async-done(((f32[2048,8192]{1,0:T(8,128)}), f32[64,8192]{1,0:T(8,128)}) %reduce-scatter.10.cloned.1.call-update) | async-done | bytes 2097168
  (483 shorter events, 509.5 us)
Async XLA Ops:
  7.2 177.9 %copy-start.4 = (bf16[128,2048]{1,0:T(8,128)(2,1)S(1)}, bf16[128,2048]{1,0:T(8,128)(2,1)}, u32[]{:S(2)}) copy-start(bf16[128,2048]{1,0:T(8,128)(2,1)} %param.25) | copy-start | bytes 1572868
  7.2 177.8 %all-gather.15.cloned.1.call-start = ((), (), s32[]{:S(2)}) async-start(), calls=%async_computation.3 | async-start | bytes 4325376 | tf_op jit(solution)/shard_map/all_gather | solution.py:191
  7.9 183.1 %all-gather.19.cloned.1.call-start = ((), (), s32[]{:S(2)}) async-start(), calls=%async_computation.5 | async-start | bytes 4325376 | tf_op jit(solution)/shard_map/all_gather | solution.py:190
  8.7 209.3 %all-gather.17.cloned.1.call-start = ((), (), s32[]{:S(2)}) async-start(), calls=%async_computation.4 | async-start | bytes 8650752 | tf_op jit(solution)/shard_map/all_gather | solution.py:192
  9.4 542.2 %all-gather.31.cloned.1.call-start = ((), (), s32[]{:S(2)}) async-start(), calls=%async_computation.11 | async-start | bytes 18874368 | tf_op jit(solution)/shard_map/all_gather | solution.py:21
  115.9 64.8 %copy-start.49 = (bf16[2048,16]{0,1:T(8,128)(2,1)}, bf16[2048,16]{0,1:T(8,128)(2,1)S(1)}, u32[]{:S(2)}) copy-start(bf16[2048,16]{0,1:T(8,128)(2,1)S(1)} %reshape.490) | copy-start | bytes 196612
  115.9 516.8 %copy-start.35 = (f32[2048]{0:T(1024)}, f32[2048]{0:T(1024)S(1)}, u32[]{:S(2)}) copy-start(f32[2048]{0:T(1024)S(1)} %convert_element_type.189) | copy-start | bytes 24580
  180.7 452.0 %copy-start.55 = (f32[128]{0:T(128)}, f32[128]{0:T(128)S(1)}, u32[]{:S(2)}) copy-start(f32[128]{0:T(128)S(1)} %fusion.123) | copy-start | bytes 1540
  327.4 305.3 %all-gather.21.cloned.1.call-start = ((), (), s32[]{:S(2)}) async-start(), calls=%async_computation.6 | async-start | bytes 8650752 | tf_op jit(solution)/shard_map/all_gather | solution.py:193
  328.0 383.5 %all-gather.23.cloned.1.call-start = ((), (), s32[]{:S(2)}) async-start(), calls=%async_computation.7 | async-start | bytes 8650752 | tf_op jit(solution)/shard_map/all_gather | solution.py:245
  328.6 527.4 %all-gather.25.cloned.1.call-start = ((), (), s32[]{:S(2)}) async-start(), calls=%async_computation.8 | async-start | bytes 23789568 | tf_op jit(solution)/shard_map/all_gather | solution.py:249
  329.4 672.3 %all-gather.27.cloned.1.call-start = ((), (), s32[]{:S(2)}) async-start(), calls=%async_computation.9 | async-start | bytes 23789568 | tf_op jit(solution)/shard_map/all_gather | solution.py:250
  330.1 817.3 %all-gather.29.cloned.1.call-start = ((), (), s32[]{:S(2)}) async-start(), calls=%async_computation.10 | async-start | bytes 23789568 | tf_op jit(solution)/shard_map/all_gather | solution.py:258
  330.8 1097.1 %all-gather.33.cloned.1.call-start = ((), (), s32[]{:S(2)}) async-start(), calls=%async_computation.12 | async-start | bytes 18874368 | tf_op jit(solution)/shard_map/all_gather | solution.py:21
  374.8 824.8 %copy-start.65 = (f32[128]{0:T(128)}, f32[128]{0:T(128)S(1)}, u32[]{:S(2)}) copy-start(f32[128]{0:T(128)S(1)} %compare_convert_fusion.4) | copy-start | bytes 1540
  640.7 77.2 %copy-start.32 = (bf16[128,4,512]{0,2,1:T(8,128)(2,1)}, bf16[128,4,512]{0,2,1:T(8,128)(2,1)S(1)}, u32[]{:S(2)}) copy-start(bf16[128,4,512]{0,2,1:T(8,128)(2,1)S(1)} %get-tuple-element.1089) | copy-start | bytes 1572868
  717.9 470.0 %copy-start.8 = (f32[128,2048]{1,0:T(8,128)}, f32[128,2048]{1,0:T(8,128)S(1)}, u32[]{:S(2)}) copy-start(f32[128,2048]{1,0:T(8,128)S(1)} %get-tuple-element.1092) | copy-start | bytes 3145732
  718.1 283.6 %copy-start.16 = (bf16[128,2048]{1,0:T(8,128)(2,1)}, bf16[128,2048]{1,0:T(8,128)(2,1)S(1)}, u32[]{:S(2)}) copy-start(bf16[128,2048]{1,0:T(8,128)(2,1)S(1)} %multiply_convert_fusion.3) | copy-start | bytes 1572868
  868.5 279.0 %copy-start.37 = (bf16[128,2048]{1,0:T(8,128)(2,1)S(1)}, bf16[128,2048]{1,0:T(8,128)(2,1)}, u32[]{:S(2)}) copy-start(bf16[128,2048]{1,0:T(8,128)(2,1)} %param.27) | copy-start | bytes 1572868
  1203.0 640.2 %reduce-scatter.14.cloned.1.call-start = ((), (), s32[]{:S(2)}) async-start(), calls=%async_computation.15 | async-start | bytes 540672
  1576.0 91.3 %copy-start.57 = (bf16[128,16]{0,1:T(8,128)(2,1)}, bf16[128,16]{0,1:T(8,128)(2,1)S(1)}, u32[]{:S(2)}) copy-start(bf16[128,16]{0,1:T(8,128)(2,1)S(1)} %convolution_convert_fusion.3) | copy-start | bytes 12292
  1577.1 267.5 %reduce-scatter.12.cloned.1.call-start = ((), (), s32[]{:S(2)}) async-start(), calls=%async_computation.14 | async-start | bytes 1081344
  1578.6 2202.3 %all-reduce.15.cloned.1.call-start = ((), (), s32[]{:S(2)}) async-start(), calls=%async_computation.16 | async-start | bytes 276824064
  1667.3 3519.9 %reduce-scatter.10.cloned.1.call-start = ((), (), s32[]{:S(2)}) async-start(), calls=%async_computation.13 | async-start | bytes 69206016
  (82 other events, 794.4 us)
Sparse Core Ops, SparseCore 0:
  11.1 63.8 all-gather.14
  78.0 60.7 all-gather.18
  141.9 76.0 all-gather.16
  327.6 223.9 all-gather.30
  554.4 78.2 all-gather.20
  635.5 75.9 all-gather.22
  714.5 141.4 all-gather.24
  858.9 142.7 all-gather.26
  1004.6 142.7 all-gather.28
  1203.1 224.8 all-gather.32
  1577.2 124.0 reduce-scatter.13
  1704.1 131.7 reduce-scatter.11
  1842.3 1938.5 all-reduce.14
  3783.1 1403.9 reduce-scatter.9
where the time goes:
time: 5210 us; the launch traced here: 5200 us
  waiting for transfers between devices  4220 us (81%)
  other arithmetic  281 us (5%)
  matrix products  281 us (5%)
  blocking collectives  244 us (5%)
  local copies, waits for them, and re-layouts  134 us (3%)
    unnamed x18, waiting for transfers between devices  3340 us
    all_gather x2, waiting for transfers between devices, prefix(): everything = jax.tree.map(lambda part: lax.all_gather(part, axis), value)  338 us
    all_gather x1, waiting for transfers between devices, local(): lax.all_gather(mlp_gate_weight, ('grp', 'seq'), axis=0, tiled=True)  138 us
    all_gather x1, waiting for transfers between devices, local(): lax.all_gather(down_weight, ('grp', 'seq'), axis=0, tiled=True)  133 us
    all_gather x1, waiting for transfers between devices, local(): up_piece = lax.all_gather(mlp_up_weight, ('grp', 'seq'), axis=0, tiled=True)  133 us
  transfers between devices with their start and end apart: 14, of which 10 were waited for; matrix products, arithmetic and copies ran while one was open for 8% of the time, Pallas kernels for 0%

commit v1 on v0

v1 whole, which is shorter than its diff:
```python
import functools

import jax
import jax.numpy as jnp
import numpy as np
from jax import lax
from jax.experimental import pallas as pl
from jax.experimental.pallas import tpu as pltpu
from jax.sharding import Mesh
from jax.sharding import PartitionSpec as P

H = 4
DK = 256
DV = 512
R = 16
CHUNK = 128
LEVELS = 7
SMALL = 128
WAIT_FLOPS = 30_000_000_000
norm_eps = 1e-06
head_eps = 0.25
decay_norm = 16.0
BF = jnp.bfloat16
F32 = jnp.float32
REST = ("x", "c", "y")
OWN = ("x", "c", "z", "y")


def dot_plain(left, right):
    return jnp.dot(left, right, preferred_element_type=F32)


def dot_rows(left, right):
    return lax.dot_general(left, right, (((1,), (1,)), ((), ())), preferred_element_type=F32)


def dot_cols(left, right):
    return lax.dot_general(left, right, (((0,), (0,)), ((), ())), preferred_element_type=F32)


def split_two(value):
    high = value.astype(BF)
    return jnp.concatenate([high, (value - high.astype(F32)).astype(BF)], axis=1)


def sum_two(value):
    half = value.shape[1] // 2
    return value[:, :half] + value[:, half:]


def chunk_tables():
    t = np.arange(CHUNK)[:, None]
    j = np.arange(CHUNK)[None, :]
    parts = []
    level = np.full((CHUNK, CHUNK), -1, np.int32)
    for number in range(LEVELS):
        half = CHUNK >> (number + 1)
        middle = t // (2 * half) * (2 * half) + half - 1
        upper = t % (2 * half) >= half
        parts.append(np.where(upper, (j > middle) & (j <= t), (j > t) & (j <= middle)))
        pair = (t // (2 * half) == j // (2 * half)) & upper & (j % (2 * half) < half)
        level[pair] = number
    level[np.arange(CHUNK), np.arange(CHUNK)] = LEVELS
    parts.append(j <= t)
    parts.append(j > t)
    return np.concatenate(parts, axis=0).astype(np.float32), level


def upper_rows(number):
    half = CHUNK >> (number + 1)
    rows = lax.broadcasted_iota(jnp.int32, (CHUNK, 1), 0)
    return lax.rem(rows, 2 * half) >= half


def factors(ld_ref, sums_ref):
    exponents = sum_two(dot_plain(sums_ref[...], split_two(ld_ref[...])))
    return jnp.exp(exponents)


def rows_of(value, number):
    return value[number * CHUNK : (number + 1) * CHUNK]


def mix_forward_body(
    q_ref, k_ref, v_ref, ld_ref, aux_ref, seg_ref, sums_ref, level_ref,
    out_ref, enter_ref, score_ref, state,
):
    @pl.when(pl.program_id(0) == 0)
    def _():
        state[...] = jnp.zeros_like(state)

    factor = factors(ld_ref, sums_ref)
    query = q_ref[...].astype(F32) * DK ** (-0.5)
    key = k_ref[...].astype(F32)
    level = level_ref[...]
    aux = aux_ref[...]
    scores = jnp.where(level == LEVELS, dot_rows(query.astype(BF), k_ref[...]), 0.0)
    for number in range(LEVELS):
        part = rows_of(factor, number)
        pairs = dot_rows((query * part).astype(BF), (key * part).astype(BF))
        scores = jnp.where(level == number, pairs, scores)
    scores = jnp.where(aux[:, 2:3] == seg_ref[0], scores, 0.0).astype(BF)
    score_ref[0] = scores
    cumulative = rows_of(factor, LEVELS)
    enter = state[...].astype(BF)
    enter_ref[0] = enter
    lifted = (query * cumulative * aux[:, 0:1]).astype(BF)
    ending = (key * rows_of(factor, LEVELS + 1) * aux[:, 1:2]).astype(BF)
    out = dot_plain(scores, v_ref[...]) + dot_rows(lifted, enter)
    out_ref[...] = out.astype(out_ref.dtype)
    through = cumulative[CHUNK - 1 :] * aux[0:1, 3:4]
    state[...] = state[...] * through + dot_cols(v_ref[...], ending)


def mix_backward_body(
    q_ref, k_ref, v_ref, ld_ref, aux_ref, seg_ref, sums_ref, sums_t_ref, level_ref, level_t_ref,
    enter_ref, score_ref, do_ref,
    dq_ref, dk_ref, dv_ref, dld_ref, state,
):
    @pl.when(pl.program_id(0) == 0)
    def _():
        state[...] = jnp.zeros_like(state)

    factor = factors(ld_ref, sums_ref)
    scale = DK ** (-0.5)
    query = q_ref[...].astype(F32) * scale
    key = k_ref[...].astype(F32)
    value = v_ref[...]
    grad = do_ref[...]
    level = level_ref[...]
    level_t = level_t_ref[...]
    aux = aux_ref[...]
    same = aux[:, 2:3] == seg_ref[0]
    weight = jnp.where(same, dot_rows(grad, value), 0.0)
    weight_t = jnp.where(same, dot_rows(value, grad), 0.0)
    diagonal = jnp.sum(jnp.where(level == LEVELS, weight, 0.0), axis=1, keepdims=True)
    dq = diagonal * key
    dk = diagonal * query
    moved = []
    for number in range(LEVELS):
        part = rows_of(factor, number)
        left = jnp.concatenate(
            [
                jnp.where(level == number, weight, 0.0).astype(BF),
                jnp.where(level_t == number, weight_t, 0.0).astype(BF),
            ],
            axis=1,
        )
        right = jnp.concatenate([(key * part).astype(BF), (query * part).astype(BF)], axis=0)
        both = dot_plain(left, right) * part
        upper = upper_rows(number)
        dq = dq + jnp.where(upper, both, 0.0)
        dk = dk + jnp.where(upper, 0.0, both)
        moved.append(both * jnp.where(upper, query, key))
    cumulative = rows_of(factor, LEVELS)
    enter = enter_ref[0]
    after = state[...]
    after_low = after.astype(BF)
    lift = cumulative * aux[:, 0:1]
    finish = rows_of(factor, LEVELS + 1) * aux[:, 1:2]
    lifted = query * lift
    ending = key * finish
    from_enter = dot_plain(grad, enter)
    from_after = dot_plain(value, after_low)
    moved.append(lifted * from_enter)
    moved.append(ending * from_after)
    dq_ref[...] = ((dq + lift * from_enter) * scale).astype(dq_ref.dtype)
    dk_ref[...] = (dk + finish * from_after).astype(dk_ref.dtype)
    dv = dot_cols(score_ref[0], grad) + dot_rows(ending.astype(BF), after_low)
    dv_ref[...] = dv.astype(dv_ref.dtype)
    through = cumulative[CHUNK - 1 :] * aux[0:1, 3:4]
    passing = jnp.sum(after * enter.astype(F32), axis=0, keepdims=True) * through
    spread = sum_two(dot_plain(sums_t_ref[...], split_two(jnp.concatenate(moved, axis=0))))
    dld_ref[...] = spread + passing
    state[...] = after * through + dot_cols(grad, lifted.astype(BF))


def mix_specs(count, width, backward):
    def at(i):
        return count - 1 - i if backward else i

    def tokens(columns):
        return pl.BlockSpec((CHUNK, columns), lambda i: (at(i), 0))

    def chunks(rows, columns):
        return pl.BlockSpec((1, rows, columns), lambda i: (at(i), 0, 0))

    def whole(rows, columns):
        return pl.BlockSpec((rows, columns), lambda i: (0, 0))

    return tokens, chunks, whole


def mix_forward(query, key, value, log_decay, aux, seg_rows):
    total, width = value.shape
    count = total // CHUNK
    sums, level = chunk_tables()
    tokens, chunks, whole = mix_specs(count, width, False)
    return pl.pallas_call(
        mix_forward_body,
        grid=(count,),
        in_specs=[
            tokens(DK), tokens(DK), tokens(width), tokens(DK), tokens(aux.shape[1]),
            chunks(1, CHUNK), whole(*sums.shape), whole(CHUNK, CHUNK),
        ],
        out_specs=[tokens(width), chunks(width, DK), chunks(CHUNK, CHUNK)],
        out_shape=[
            jax.ShapeDtypeStruct((total, width), BF),
            jax.ShapeDtypeStruct((count, width, DK), BF),
            jax.ShapeDtypeStruct((count, CHUNK, CHUNK), BF),
        ],
        scratch_shapes=[pltpu.VMEM((width, DK), F32)],
        compiler_params=pltpu.CompilerParams(
            dimension_semantics=("arbitrary",), vmem_limit_bytes=32 * 1024 * 1024
        ),
        cost_estimate=pl.CostEstimate(
            flops=total * 2 * (8 * CHUNK * DK + 2 * width * DK + CHUNK * width + 18 * CHUNK * DK),
            bytes_accessed=total * 4096, transcendentals=total * 9 * DK,
        ),
        name="mix_forward",
    )(query, key, value, log_decay, aux, seg_rows, jnp.asarray(sums, BF), jnp.asarray(level))


def mix_backward(query, key, value, log_decay, aux, seg_rows, enter, scores, grad):
    total, width = value.shape
    count = total // CHUNK
    sums, level = chunk_tables()
    tokens, chunks, whole = mix_specs(count, width, True)
    return pl.pallas_call(
        mix_backward_body,
        grid=(count,),
        in_specs=[
            tokens(DK), tokens(DK), tokens(width), tokens(DK), tokens(aux.shape[1]),
            chunks(1, CHUNK), whole(*sums.shape), whole(*sums.shape[::-1]),
            whole(CHUNK, CHUNK), whole(CHUNK, CHUNK),
            chunks(width, DK), chunks(CHUNK, CHUNK), tokens(width),
        ],
        out_specs=[tokens(DK), tokens(DK), tokens(width), tokens(DK)],
        out_shape=[
            jax.ShapeDtypeStruct((total, DK), BF),
            jax.ShapeDtypeStruct((total, DK), BF),
            jax.ShapeDtypeStruct((total, width), BF),
            jax.ShapeDtypeStruct((total, DK), F32),
        ],
        scratch_shapes=[pltpu.VMEM((width, DK), F32)],
        compiler_params=pltpu.CompilerParams(
            dimension_semantics=("arbitrary",), vmem_limit_bytes=48 * 1024 * 1024
        ),
        cost_estimate=pl.CostEstimate(
            flops=total * 2 * (14 * CHUNK * DK + 4 * width * DK + CHUNK * width + 36 * CHUNK * DK),
            bytes_accessed=total * 6144, transcendentals=total * 9 * DK,
        ),
        name="mix_backward",
    )(
        query, key, value, log_decay, aux, seg_rows, jnp.asarray(sums, BF),
        jnp.asarray(np.ascontiguousarray(sums.T), BF), jnp.asarray(level),
        jnp.asarray(np.ascontiguousarray(level.T)), enter, scores, grad,
    )


def remote(source, target, send, arrive, axis, place):
    return pltpu.make_async_remote_copy(
        src_ref=source, dst_ref=target, send_sem=send, recv_sem=arrive,
        device_id={axis: place}, device_id_type=pl.DeviceIdType.MESH,
    )


def greet_line(axis, count):
    me = lax.axis_index(axis)
    barrier = pltpu.get_barrier_semaphore()

    @pl.when(me > 0)
    def _():
        pl.semaphore_signal(
            barrier, inc=1, device_id={axis: me - 1}, device_id_type=pl.DeviceIdType.MESH
        )

    @pl.when(me < count - 1)
    def _():
        pl.semaphore_signal(
            barrier, inc=1, device_id={axis: me + 1}, device_id_type=pl.DeviceIdType.MESH
        )

    pl.semaphore_wait(barrier, jnp.where((me > 0) & (me < count - 1), 2, 1))


def gather_body(axis, count, x_ref, out_ref, send, arrive, local_sem):
    me = lax.axis_index(axis)
    own = x_ref.shape[0]
    greet_line(axis, count)

    def block(index):
        return out_ref.at[pl.ds(pl.multiple_of(index * own, own), own)]

    def hop(direction, step):
        index = me - step if direction == 0 else me + step
        source = x_ref if step == 0 else block(index)
        return remote(
            source, block(index), send.at[direction, step], arrive.at[direction, step],
            axis, me + 1 if direction == 0 else me - 1,
        )

    def landed(direction, step):
        index = me - 1 - step if direction == 0 else me + 1 + step
        return remote(
            block(index), block(index), send.at[direction, step], arrive.at[direction, step],
            axis, me + 1 if direction == 0 else me - 1,
        )

    mine = pltpu.make_async_copy(x_ref, block(me), local_sem)
    mine.start()
    for step in range(count):
        if step > 0:

            @pl.when(me - step >= 0)
            def _():
                landed(0, step - 1).wait_recv()

        if step < count - 1:

            @pl.when((me - step >= 0) & (me < count - 1))
            def _():
                hop(0, step).start()

        if step > 0:

            @pl.when(me + step <= count - 1)
            def _():
                landed(1, step - 1).wait_recv()

        if step < count - 1:

            @pl.when((me + step <= count - 1) & (me > 0))
            def _():
                hop(1, step).start()

    for step in range(count - 1):

        @pl.when((me - step >= 0) & (me < count - 1))
        def _():
            hop(0, step).wait_send()

        @pl.when((me + step <= count - 1) & (me > 0))
        def _():
            hop(1, step).wait_send()

    mine.wait()


def gather_line(block, axis, number):
    count = lax.axis_size(axis)
    rows, columns = block.shape
    return pl.pallas_call(
        functools.partial(gather_body, axis, count),
        in_specs=[pl.BlockSpec(memory_space=pl.ANY)],
        out_specs=pl.BlockSpec(memory_space=pl.ANY),
        out_shape=jax.ShapeDtypeStruct((count * rows, columns), block.dtype),
        scratch_shapes=[
            pltpu.SemaphoreType.DMA((2, count - 1)),
            pltpu.SemaphoreType.DMA((2, count - 1)),
            pltpu.SemaphoreType.DMA,
        ],
        compiler_params=pltpu.CompilerParams(collective_id=number, has_side_effects=True),
        cost_estimate=pl.CostEstimate(
            flops=WAIT_FLOPS, bytes_accessed=count * rows * columns * 4, transcendentals=0
        ),
        name="gather_line",
    )(block)


def scatter_body(axis, count, x_ref, out_ref, up, down, send, arrive):
    me = lax.axis_index(axis)
    own = out_ref.shape[0]
    greet_line(axis, count)

    def part(index):
        return x_ref.at[pl.ds(pl.multiple_of(index * own, own), own)]

    def hop(direction, number, source):
        held = (up, down)[direction].at[number]
        return remote(
            source, held, send.at[direction, number], arrive.at[direction, number],
            axis, me + 1 if direction == 0 else me - 1,
        )

    def stage(direction, number):
        target = count - 1 - number if direction == 0 else number
        first = me == 0 if direction == 0 else me == count - 1
        passed = me < target if direction == 0 else me > target
        held = (up, down)[direction].at[number]

        @pl.when(first)
        def _():
            hop(direction, number, part(target)).start()

        @pl.when(jnp.logical_not(first) & (passed | (me == target)))
        def _():
            hop(direction, number, held).wait_recv()

        @pl.when(jnp.logical_not(first) & passed)
        def _():
            held[...] = (held[...].astype(F32) + part(target)[...].astype(F32)).astype(BF)
            hop(direction, number, held).start()

    for order in (0, 1):

        @pl.when((me >= count // 2) == (order == 1))
        def _():
            for number in range(count - 1):
                stage(order, number)
                stage(1 - order, number)

    out_ref[...] = part(me)[...].astype(F32)
    for number in range(count - 1):

        @pl.when(me == count - 1 - number)
        def _():
            out_ref[...] += up[number].astype(F32)

        @pl.when(me == number)
        def _():
            out_ref[...] += down[number].astype(F32)

    for number in range(count - 1):

        @pl.when(me < count - 1 - number)
        def _():
            hop(0, number, up.at[number]).wait_send()

        @pl.when(me > number)
        def _():
            hop(1, number, down.at[number]).wait_send()


def scatter_line(partial, axis, number):
    count = lax.axis_size(axis)
    rows, columns = partial.shape
    own = rows // count
    return pl.pallas_call(
        functools.partial(scatter_body, axis, count),
        in_specs=[pl.BlockSpec(memory_space=pltpu.VMEM)],
        out_specs=pl.BlockSpec(memory_space=pltpu.VMEM),
        out_shape=jax.ShapeDtypeStruct((own, columns), F32),
        scratch_shapes=[
            pltpu.VMEM((count - 1, own, columns), BF),
            pltpu.VMEM((count - 1, own, columns), BF),
            pltpu.SemaphoreType.DMA((2, count - 1)),
            pltpu.SemaphoreType.DMA((2, count - 1)),
        ],
        compiler_params=pltpu.CompilerParams(
            collective_id=number, has_side_effects=True, vmem_limit_bytes=32 * 1024 * 1024
        ),
        cost_estimate=pl.CostEstimate(
            flops=WAIT_FLOPS, bytes_accessed=rows * columns * 4, transcendentals=0
        ),
        name="scatter_line",
    )(partial)


def swap_body(axis, count, x_ref, out_ref, send, arrive, local_sem):
    me = lax.axis_index(axis)
    barrier = pltpu.get_barrier_semaphore()
    for away in range(1, count):
        pl.semaphore_signal(
            barrier, inc=1, device_id={axis: lax.rem(me + away, count)},
            device_id_type=pl.DeviceIdType.MESH,
        )
    pl.semaphore_wait(barrier, count - 1)
    mine = pltpu.make_async_copy(x_ref.at[me], out_ref.at[me], local_sem)
    mine.start()

    def hop(away):
        peer = lax.rem(me + away, count)
        return remote(
            x_ref.at[peer], out_ref.at[me], send.at[away - 1], arrive.at[away - 1], axis, peer
        )

    def landed(away):
        peer = lax.rem(me + count - away, count)
        return remote(
            x_ref.at[peer], out_ref.at[peer], send.at[away - 1], arrive.at[away - 1], axis, peer
        )

    for away in range(1, count):
        hop(away).start()
    for away in range(1, count):
        landed(away).wait_recv()
    for away in range(1, count):
        hop(away).wait_send()
    mine.wait()


def swap_blocks(value, axis, number):
    count = lax.axis_size(axis)
    return pl.pallas_call(
        functools.partial(swap_body, axis, count),
        in_specs=[pl.BlockSpec(memory_space=pl.ANY)],
        out_specs=pl.BlockSpec(memory_space=pl.ANY),
        out_shape=jax.ShapeDtypeStruct(value.shape, value.dtype),
        scratch_shapes=[
            pltpu.SemaphoreType.DMA((count - 1,)),
            pltpu.SemaphoreType.DMA((count - 1,)),
            pltpu.SemaphoreType.DMA,
        ],
        compiler_params=pltpu.CompilerParams(collective_id=number, has_side_effects=True),
        cost_estimate=pl.CostEstimate(
            flops=WAIT_FLOPS // 2, bytes_accessed=value.size * 4, transcendentals=0
        ),
        name="swap_blocks",
    )(value)


def local(
    tokens, doc_lengths, cotangent, attn_gain, query_weight, key_weight, value_weight, gate_weight,
    rank_in, rank_out, decay_bias, head_gain, out_weight, mlp_gain, mlp_gate_weight,
    mlp_up_weight, down_weight,
):
    own, width = tokens.shape
    rows = query_weight.shape[0]
    X, C, Z, Y = (lax.axis_size(name) for name in OWN)
    z = lax.axis_index("z")
    group = own * Z
    total = group * Y
    ff = down_weight.shape[1] // Z
    dvp = DV // Y

    def blocked(value):
        lead = value.shape[:-1]
        cut = value.reshape(lead + (X, C, Z, Y, rows))
        return jnp.swapaxes(cut, -3, -2).reshape(lead + (width,))

    def unblocked(value):
        lead = value.shape[:-1]
        cut = value.reshape(lead + (X, C, Y, Z, rows))
        return jnp.swapaxes(cut, -3, -2).reshape(lead + (width,))

    def cut_columns(weight):
        return jnp.swapaxes(weight.reshape(rows, Z, weight.shape[1] // Z), 0, 1)

    def pad_rows(value):
        flat = value.reshape(value.shape[0], -1)
        return jnp.pad(flat, ((0, rows - flat.shape[0]), (0, 0)))

    numbers = iter(range(32))

    def swap_z(value):
        return swap_blocks(value, "z", next(numbers))

    def swap_y(value):
        return swap_blocks(value, "y", next(numbers))

    def gather_z(value):
        return gather_line(value, "z", next(numbers))

    def scatter_z(value):
        return scatter_line(value.astype(BF), "z", next(numbers))

    def to_sequence(value):
        cut = value.reshape(Y, Z, own, value.shape[-1])
        return jnp.swapaxes(cut, 0, 1).reshape(total, value.shape[-1])

    def from_sequence(value):
        cut = value.reshape(Z, Y, own, value.shape[-1])
        return jnp.swapaxes(cut, 0, 1).reshape(Y, group, value.shape[-1])

    def gather_rest(value):
        return lax.all_gather(value, REST, axis=0, tiled=True)

    small = jnp.concatenate(
        [
            rank_in, pad_rows(attn_gain), pad_rows(mlp_gain), pad_rows(rank_out),
            pad_rows(decay_bias), pad_rows(head_gain),
        ],
        axis=1,
    )
    small = jnp.pad(small, ((0, 0), (0, SMALL - small.shape[1])))
    first = jnp.concatenate(
        [cut_columns(w) for w in (query_weight, key_weight, value_weight, gate_weight)]
        + [jnp.broadcast_to(small[None], (Z,) + small.shape)],
        axis=2,
    )
    input_weights = gather_rest(swap_z(first).reshape(Z * rows, -1))
    second = swap_z(
        jnp.concatenate(
            [cut_columns(w) for w in (out_weight, mlp_gate_weight, mlp_up_weight, down_weight)],
            axis=2,
        )
    ).reshape(Z * rows, -1)
    out_piece = gather_rest(second[:, :DV])
    mlp_piece = gather_rest(second[:, DV : DV + 2 * ff])
    down_piece = gather_rest(second[:, DV + 2 * ff :])

    own_tokens = blocked(tokens)
    group_tokens = gather_z(own_tokens)
    group_cotangent = gather_z(blocked(cotangent))

    projected = 2 * DK + 2 * DV
    small_all = input_weights[:, projected:].astype(F32)

    def device_rows(value, count):
        cut = value.reshape(X, C, Y, Z, rows, -1)[:, :, :, :, : rows // count]
        return jnp.swapaxes(cut, 2, 3).reshape(width // count, -1)

    attn_gain_all = small_all[:, R]
    mlp_gain_all = small_all[:, R + 1]
    rank_out_all = device_rows(small_all[:, R + 2 : 2 * R + 2], width // (H * DK))
    bias_all = device_rows(small_all[:, 2 * R + 2 : 2 * R + 3], width // (H * DK))
    head_gain_all = device_rows(small_all[:, 2 * R + 3 : 2 * R + 4], width // DV)[:, 0]
    rank_out_z = lax.dynamic_slice_in_dim(rank_out_all, z * DK, DK).astype(BF)
    bias_z = lax.dynamic_slice_in_dim(bias_all, z * DK, DK)[:, 0]

    rows_in = group_tokens.astype(F32)
    scale_in = lax.rsqrt(jnp.mean(rows_in * rows_in, axis=1, keepdims=True) + norm_eps)
    normed_in = (rows_in * scale_in * attn_gain_all).astype(BF)
    heads = dot_plain(normed_in, input_weights)
    out_gate = heads[:, 2 * DK + DV : projected]
    low = heads.astype(BF)
    shared = jnp.concatenate([low[:, : 2 * DK], low[:, projected:]], axis=1)
    values = jnp.swapaxes(low[:, 2 * DK : 2 * DK + DV].reshape(group, Y, dvp), 0, 1)
    sent = jnp.concatenate([jnp.broadcast_to(shared[None], (Y,) + shared.shape), values], axis=2)
    sequence = to_sequence(swap_y(sent))
    queries = sequence[:, :DK]
    keys = sequence[:, DK : 2 * DK]
    rank_low = sequence[:, 2 * DK : 2 * DK + R]
    value_part = sequence[:, 2 * DK + SMALL :]
    decay_logit = dot_rows(rank_low, rank_out_z) + bias_z
    log_decay = jax.nn.log_sigmoid(decay_logit) / decay_norm

    doc_ends = jnp.cumsum(doc_lengths[0])
    positions = lax.iota(jnp.int32, total)
    segments = jnp.sum((doc_ends[None, :] <= positions[:, None]).astype(jnp.int32), axis=1)
    cut = segments.reshape(-1, CHUNK)
    last = cut[:, CHUNK - 1 :]
    before = jnp.concatenate([jnp.full((1, 1), -1, jnp.int32), last[:-1]], axis=0)
    aux = jnp.stack(
        [cut == before, cut == last, cut, jnp.broadcast_to(last == before, cut.shape)], axis=-1
    )
    aux = aux.reshape(total, 4).astype(F32)
    seg_rows = cut.astype(F32)[:, None, :]

    mixed_part, enter, scores = mix_forward(queries, keys, value_part, log_decay, aux, seg_rows)
    mixed = jnp.swapaxes(swap_y(from_sequence(mixed_part)), 0, 1).reshape(group, DV).astype(F32)

    head_scale = lax.rsqrt(jnp.mean(mixed * mixed, axis=1, keepdims=True) + head_eps)
    head_hat = mixed * head_scale
    head_out = head_hat * head_gain_all
    sig_out = jax.nn.sigmoid(out_gate)
    silu_out = out_gate * sig_out
    gated = (head_out * silu_out).astype(BF)
    residual = own_tokens.astype(F32) + scatter_z(dot_rows(gated, out_piece))
    scale_mid = lax.rsqrt(jnp.mean(residual * residual, axis=1, keepdims=True) + norm_eps)
    hat_mid = residual * scale_mid
    normed_mlp = gather_z((hat_mid * mlp_gain_all).astype(BF))

    both_pre = dot_plain(normed_mlp, mlp_piece)
    gate_pre = both_pre[:, :ff]
    up_pre = both_pre[:, ff:]
    sig_gate = jax.nn.sigmoid(gate_pre)
    silu_gate = gate_pre * sig_gate
    hidden = (silu_gate * up_pre).astype(BF)
    grad_hidden = dot_plain(group_cotangent, down_piece)
    grad_gate = (grad_hidden * up_pre * sig_gate * (1.0 + gate_pre * (1.0 - sig_gate))).astype(BF)
    grad_up = (grad_hidden * silu_gate).astype(BF)
    grad_both = jnp.concatenate([grad_gate, grad_up], axis=1)
    grad_normed_mlp = scatter_z(dot_rows(grad_both, mlp_piece))
    layer_out = residual + scatter_z(dot_rows(hidden, down_piece))

    mlp_sums = lax.psum_scatter(
        jnp.concatenate(
            [dot_cols(normed_mlp, grad_both), dot_cols(group_cotangent, hidden)], axis=1
        ).astype(BF),
        REST, scatter_dimension=0, tiled=True,
    )
    mlp_rows = swap_z(mlp_sums.reshape(Z, rows, 3 * ff)).astype(F32)

    mlp_gain_part = jnp.sum(grad_normed_mlp * hat_mid, axis=0)
    scaled = grad_normed_mlp * mlp_gain_all
    grad_residual = blocked(cotangent).astype(F32) + scale_mid * (
        scaled - hat_mid * jnp.mean(scaled * hat_mid, axis=1, keepdims=True)
    )
    grad_branch = gather_z(grad_residual.astype(BF))
    grad_gated = dot_plain(grad_branch, out_piece)
    grad_head = grad_gated * silu_out
    head_gain_part = jnp.sum(grad_head * head_hat, axis=0)
    from_head = grad_head * head_gain_all
    grad_mixed = head_scale * (
        from_head - head_hat * jnp.mean(from_head * head_hat, axis=1, keepdims=True)
    )
    grad_out_gate = (grad_gated * head_out * sig_out * (1.0 + out_gate * (1.0 - sig_out))).astype(BF)
    grad_part = to_sequence(
        swap_y(jnp.swapaxes(grad_mixed.astype(BF).reshape(group, Y, dvp), 0, 1))
    )
    dq, dk, dv, dld = mix_backward(
        queries, keys, value_part, log_decay, aux, seg_rows, enter, scores, grad_part
    )
    dlogit = (dld * jax.nn.sigmoid(-decay_logit) / decay_norm).astype(BF)
    back = swap_y(from_sequence(jnp.concatenate([dq, dk, dlogit, dv], axis=1)))
    summed = jnp.sum(back[:, :, : 3 * DK].astype(F32), axis=0).astype(BF)
    grad_value = jnp.swapaxes(back[:, :, 3 * DK :], 0, 1).reshape(group, DV)
    grad_logit = summed[:, 2 * DK :]
    bias_part = jnp.sum(grad_logit.astype(F32), axis=0)
    rank_low_group = low[:, projected : projected + R]
    rank_out_part = dot_cols(grad_logit, rank_low_group)
    grad_rank = dot_plain(grad_logit, rank_out_z).astype(BF)
    grad_heads = jnp.concatenate(
        [
            summed[:, : 2 * DK], grad_value, grad_out_gate,
            jnp.pad(grad_rank, ((0, 0), (0, SMALL - R))),
        ],
        axis=1,
    )
    grad_normed_in = scatter_z(dot_rows(grad_heads, input_weights))
    rows_own = own_tokens.astype(F32)
    scale_own = lax.rsqrt(jnp.mean(rows_own * rows_own, axis=1, keepdims=True) + norm_eps)
    hat_own = rows_own * scale_own
    attn_gain_part = jnp.sum(grad_normed_in * hat_own, axis=0)
    scaled_in = grad_normed_in * attn_gain_all
    tokens_grad = grad_residual + scale_own * (
        scaled_in - hat_own * jnp.mean(scaled_in * hat_own, axis=1, keepdims=True)
    )

    def to_device_rows(value, count):
        cut = value.reshape(X, C, Z, Y, rows // count, -1)
        cut = jnp.swapaxes(cut, 2, 3)
        cut = jnp.pad(cut, ((0, 0),) * 4 + ((0, rows - rows // count), (0, 0)))
        return cut.reshape(width, -1)

    def at_head(value):
        return lax.dynamic_update_slice_in_dim(
            jnp.zeros((H * DK, value.shape[1]), F32), value, z * DK, 0
        )

    weight_part = dot_cols(normed_in, grad_heads)
    small_part = jnp.concatenate(
        [
            weight_part[:, projected : projected + R],
            attn_gain_part[:, None],
            mlp_gain_part[:, None],
            to_device_rows(at_head(rank_out_part), width // (H * DK)),
            to_device_rows(at_head(bias_part[:, None]), width // (H * DK)),
            to_device_rows(head_gain_part[:, None], width // DV),
        ],
        axis=1,
    )
    small_part = jnp.pad(small_part, ((0, 0), (0, SMALL - small_part.shape[1])))
    attn_sums = lax.psum_scatter(
        jnp.concatenate(
            [weight_part[:, :projected], dot_cols(grad_branch, gated), small_part], axis=1
        ).astype(BF),
        REST, scatter_dimension=0, tiled=True,
    )
    attn_rows = swap_z(attn_sums.reshape(Z, rows, -1)).astype(F32)

    def joined(value):
        return jnp.swapaxes(value, 0, 1).reshape(rows, -1)

    small_rows = jnp.sum(attn_rows[:, :, projected + DV :], axis=0)
    return (
        unblocked(layer_out),
        unblocked(tokens_grad),
        small_rows[:, R],
        joined(attn_rows[:, :, :DK]),
        joined(attn_rows[:, :, DK : 2 * DK]),
        joined(attn_rows[:, :, 2 * DK : 2 * DK + DV]),
        joined(attn_rows[:, :, 2 * DK + DV : projected]),
        small_rows[:, :R],
        small_rows[: rows * H * DK // width, R + 2 : 2 * R + 2],
        small_rows[: rows * H * DK // width, 2 * R + 2],
        small_rows[: rows * DV // width, 2 * R + 3],
        joined(attn_rows[:, :, projected : projected + DV]),
        small_rows[:, R + 1],
        joined(mlp_rows[:, :, :ff]),
        joined(mlp_rows[:, :, ff : 2 * ff]),
        joined(mlp_rows[:, :, 2 * ff :]),
    )


def solution(mesh):
    groups, places = mesh.shape["grp"], mesh.shape["seq"]
    wide = Mesh(mesh.devices.reshape(groups // 2, 2, H, places // H), OWN)
    split = P(OWN, None)
    line = P(OWN)
    by_sequence = P(("x", "c"), None)
    placed = (
        split, by_sequence, split, line, split, split, split, split, split, split,
        line, line, split, line, split, split, split,
    )
    return jax.shard_map(
        local,
        mesh=wide,
        in_specs=placed,
        out_specs=(
            split, split, line, split, split, split, split, split, split, line, line, split,
            line, split, split, split,
        ),
        check_vma=False,
    )
```

time: 5210 us -> 860 us (0.17)
  waiting for transfers between devices: 4220 us -> 94.9 us
  Pallas kernels: 0 us -> 559 us
  blocking collectives: 244 us -> 0 us
  other arithmetic: 281 us -> 39.1 us
  matrix products: 281 us -> 84.6 us
  local copies, waits for them, and re-layouts: 134 us -> 62.7 us
    unnamed x18 -> x6, waiting for transfers between devices: 3340 us -> 0.1 us
    all_gather x10 -> x4, waiting for transfers between devices: 882 us -> 0.06 us  [gather_rest(): return lax.all_gather(value, REST, axis=0, tiled=True)]
    pallas_call x0 -> x18, Pallas kernels: none -> 559 us  [the longest x8 240 us: swap_blocks(): pl.pallas_call(functools.partial(swap_body, axis, count), in_specs=[pl.Bl...]
    all_gather x3 -> x0, blocking collectives: 147 us -> none  [the longest x1 62.8 us: local(): low_piece = lax.all_gather(rank_out, ('grp', 'seq'), axis=0, tiled=True)]
    unnamed x3 -> x0, blocking collectives: 96.9 us -> none
    reduce_scatter x0 -> x2, waiting for transfers between devices: none -> 94.8 us  [the longest x1 84 us: local(): lax.psum_scatter(jnp.concatenate([dot_cols(normed_mlp, grad_both), dot_co...]
    dot_general x31 -> x5, matrix products: 120 us -> 34 us  [dot_plain(): return jnp.dot(left, right, preferred_element_type=F32)]
    concatenate x1 -> x7, other arithmetic: 88.6 us -> 18.2 us  [the longest x1 7.4 us: local(): jnp.concatenate([weight_part[:, :projected], dot_cols(grad_branch, gated)...]
  transfers between devices with their start and end apart: 14 -> 6, of which waited for: 10 -> 2; matrix products, arithmetic and copies ran while one was open for 8% -> 12% of each run, Pallas kernels for 0% -> 37%
where the time goes in v1:
time: 860 us; the launch traced here: 856 us
  Pallas kernels  559 us (65%)
  waiting for transfers between devices  94.9 us (11%)
  matrix products  84.6 us (10%)
  local copies, waits for them, and re-layouts  62.7 us (7%)
  other arithmetic  39.1 us (5%)
  between operations  15.8 us (2%)
    pallas_call x8, Pallas kernels, swap_blocks(): pl.pallas_call(functools.partial(swap_body, axis, count), in_specs=[pl.Bl...  240 us
    pallas_call x4, Pallas kernels, scatter_line(): pl.pallas_call(functools.partial(scatter_body, axis, count), in_specs=[pl...  161 us
    pallas_call x4, Pallas kernels, gather_line(): pl.pallas_call(functools.partial(gather_body, axis, count), in_specs=[pl....  136 us
    reduce_scatter x1, waiting for transfers between devices, local(): lax.psum_scatter(jnp.concatenate([dot_cols(normed_mlp, grad_both), dot_co...  84 us
    dot_general x5, matrix products, dot_plain(): return jnp.dot(left, right, preferred_element_type=F32)  34 us
    dot_general x5, matrix products, dot_rows(): lax.dot_general(left, right, (((1,), (1,)), ((), ())), preferred_element_...  25.9 us
    dot_general x5, matrix products, dot_cols(): lax.dot_general(left, right, (((0,), (0,)), ((), ())), preferred_element_...  24.7 us
  transfers between devices with their start and end apart: 6, of which 2 were waited for; matrix products, arithmetic and copies ran while one was open for 12% of the time, Pallas kernels for 37%

profile of v1, /device:TPU:9, one launch (start us, length us, event | category | flops | bytes accessed | tf_op | source)
XLA Modules:
  0.0 856.1 jit_solution(14278178053014341773)
XLA Ops:
  15.6 22.3 %swap_blocks.8 = bf16[4,64,1664]{2,1,0:T(8,128)(2,1)} custom-call(bf16[4,64,1664]{2,1,0:T(8,128)(2,1)} %copy-done.49), custom_call_target="tpu_custom_call" | custom-call | flops 15000000512 | bytes 1703936 | tf_op jit(solution)/shard_map/swap_blocks/pallas_call | solution.py:495
  42.2 54.0 %swap_blocks.11 = bf16[4,64,4736]{2,1,0:T(8,128)(2,1)} custom-call(bf16[4,64,4736]{2,1,0:T(8,128)(2,1)} %pad_maximum_fusion.2.x_ref), custom_call_target="tpu_custom_call" | custom-call | flops 15000000512 | bytes 4849664 | tf_op jit(solution)/shard_map/swap_blocks/pallas_call | solution.py:495
  107.5 33.0 %gather_line.4 = bf16[512,2048]{1,0:T(8,128)(2,1)} custom-call(bf16[128,2048]{1,0:T(8,128)(2,1)} %copy.367.x_ref), custom_call_target="tpu_custom_call" | custom-call | flops 30000001024 | bytes 4194304 | tf_op jit(solution)/shard_map/gather_line/pallas_call | solution.py:353
  142.8 34.0 %gather_line.6 = bf16[512,2048]{1,0:T(8,128)(2,1)} custom-call(bf16[128,2048]{1,0:T(8,128)(2,1)} %copy.394.x_ref), custom_call_target="tpu_custom_call" | custom-call | flops 30000001024 | bytes 4194304 | tf_op jit(solution)/shard_map/gather_line/pallas_call | solution.py:353
  178.1 8.9 %fusion.43 = (bf16[512,1664]{1,0:T(8,128)(2,1)S(1)}, f32[512,1664]{1,0:T(8,128)}) fusion(bf16[2048,1664]{0,1:T(8,128)(2,1)} %all-gather.5.cloned.1.call-done, bf16[512,2048]{1,0:T(8,128)(2,1)S(1)} %copy-done.29, f32[2048]{0:T(1024)S(1)} %bitcast.265, f32[512]{0:T(512)S(1)} %add_rsqrt_fusion.1), kind=kOutput, calls=%fused_computation.133 | convolution fusion | flops 3494707200 | bytes 14034944 | tf_op jit(solution)/shard_map/dot_general | solution.py:30
  191.0 30.2 %swap_blocks.9 = bf16[2,512,896]{2,1,0:T(8,128)(2,1)} custom-call(bf16[2,512,896]{2,1,0:T(8,128)(2,1)} %pad_maximum_fusion.6.x_ref), custom_call_target="tpu_custom_call" | custom-call | flops 15000000512 | bytes 3670016 | tf_op jit(solution)/shard_map/swap_blocks/pallas_call | solution.py:495
  224.9 7.8 mix_forward.1
  233.9 13.0 %swap_blocks.10 = bf16[2,512,256]{2,1,0:T(8,128)(2,1)} custom-call(bf16[2,512,256]{2,1,0:T(8,128)(2,1)} %bitcast.246), custom_call_target="tpu_custom_call" | custom-call | flops 15000000512 | bytes 1048576 | tf_op jit(solution)/shard_map/swap_blocks/pallas_call | solution.py:495
  254.1 42.5 %scatter_line.4 = f32[128,2048]{1,0:T(8,128)S(1)} custom-call(bf16[512,2048]{1,0:T(8,128)(2,1)S(1)} %convolution_convert_fusion.6.x_ref), custom_call_target="tpu_custom_call" | custom-call | flops 30000001024 | bytes 4194304 | tf_op jit(solution)/shard_map/scatter_line/pallas_call | solution.py:439
  297.9 37.2 %gather_line.5 = bf16[512,2048]{1,0:T(8,128)(2,1)} custom-call(bf16[128,2048]{1,0:T(8,128)(2,1)} %multiply_convert_fusion.6.x_ref), custom_call_target="tpu_custom_call" | custom-call | flops 30000001024 | bytes 4194304 | tf_op jit(solution)/shard_map/gather_line/pallas_call | solution.py:353
  335.1 12.6 %fusion.44 = f32[512,2816]{1,0:T(8,128)} fusion(bf16[512,2048]{1,0:T(8,128)(2,1)} %gather_line.5, bf16[2048,2816]{1,0:T(8,128)(2,1)} %all-gather.9.cloned.1.call-done), kind=kOutput, calls=%fused_computation.134 | convolution fusion | flops 5905580032 | bytes 19398656 | tf_op jit(solution)/shard_map/dot_general | solution.py:30
  347.8 8.8 %multiply_convert_fusion.1 = (bf16[512,1408]{1,0:T(8,128)(2,1)S(1)}, bf16[512,1408]{1,0:T(8,128)(2,1)S(1)}, bf16[512,1408]{1,0:T(8,128)(2,1)}) fusion(f32[512,2816]{1,0:T(8,128)} %fusion.44, bf16[512,2048]{1,0:T(8,128)(2,1)S(1)} %copy-done.65, bf16[2048,1408]{1,0:T(8,128)(2,1)} %all-gather.11.cloned.1.call-done), kind=kOutput, calls=%fused_computation.24 | convolution fusion | flops 2963603456 | bytes 17956864 | tf_op jit(solution)/shard_map/dot_general | solution.py:30
  363.0 39.2 %scatter_line.6 = f32[128,2048]{1,0:T(8,128)S(1)} custom-call(bf16[512,2048]{1,0:T(8,128)(2,1)S(1)} %convolution_convert_fusion.5.x_ref), custom_call_target="tpu_custom_call" | custom-call | flops 30000001024 | bytes 4194304 | tf_op jit(solution)/shard_map/scatter_line/pallas_call | solution.py:439
  404.4 32.3 %gather_line.7 = bf16[512,2048]{1,0:T(8,128)(2,1)} custom-call(bf16[128,2048]{1,0:T(8,128)(2,1)} %fusion.40.x_ref), custom_call_target="tpu_custom_call" | custom-call | flops 30000001024 | bytes 4194304 | tf_op jit(solution)/shard_map/gather_line/pallas_call | solution.py:353
  446.2 10.8 %swap_blocks.12 = bf16[2,512,256]{2,1,0:T(8,128)(2,1)} custom-call(bf16[2,512,256]{2,1,0:T(8,128)(2,1)} %bitcast.247), custom_call_target="tpu_custom_call" | custom-call | flops 15000000512 | bytes 1048576 | tf_op jit(solution)/shard_map/swap_blocks/pallas_call | solution.py:495
  458.1 13.8 %mix_backward.1 = (bf16[1024,256]{1,0:T(8,128)(2,1)S(1)}, bf16[1024,256]{1,0:T(8,128)(2,1)S(1)}, bf16[1024,256]{1,0:T(8,128)(2,1)S(1)}, f32[1024,256]{1,0:T(8,128)}) custom-call(bf16[1024,256]{1,0:T(8,128)(2,1)S(1)} %copy-done.7, bf16[1024,256]{1,0:T(8,128)(2,1)S(1)} %copy-done.5, bf16[1024,256]{1,0:T(8,128)(2,1)S(1)} %copy-done.3, f32[1024,256]{1,0:T(8,128)} %copy-done.16, ...), custom_call_target="tpu_custom_call" | custom-call | flops 3959422976 | bytes 6291456 | tf_op jit(solution)/shard_map/mix_backward/pallas_call | solution.py:229
  475.2 32.9 %swap_blocks.13 = bf16[2,512,1024]{2,1,0:T(8,128)(2,1)} custom-call(bf16[2,512,1024]{2,1,0:T(8,128)(2,1)} %bitcast.223), custom_call_target="tpu_custom_call" | custom-call | flops 15000000512 | bytes 4194304 | tf_op jit(solution)/shard_map/swap_blocks/pallas_call | solution.py:495
  535.8 39.6 %scatter_line.7 = f32[128,2048]{1,0:T(8,128)S(1)} custom-call(bf16[512,2048]{1,0:T(8,128)(2,1)S(1)} %convolution_convert_fusion.4.x_ref), custom_call_target="tpu_custom_call" | custom-call | flops 30000001024 | bytes 4194304 | tf_op jit(solution)/shard_map/scatter_line/pallas_call | solution.py:439
  590.4 8.3 convolution_convert_fusion
  613.6 39.6 %scatter_line.5 = f32[128,2048]{1,0:T(8,128)S(1)} custom-call(bf16[512,2048]{1,0:T(8,128)(2,1)S(1)} %convolution_convert_fusion.7.x_ref), custom_call_target="tpu_custom_call" | custom-call | flops 30000001024 | bytes 4194304 | tf_op jit(solution)/shard_map/scatter_line/pallas_call | solution.py:439
  659.9 10.8 %reduce-scatter.3.cloned.1.call-done = bf16[256,2176]{0,1:T(8,128)(2,1)} async-done(((bf16[2048,2176]{0,1:T(8,128)(2,1)}), bf16[256,2176]{0,1:T(8,128)(2,1)}) %reduce-scatter.3.cloned.1.call-update) | async-done | bytes 1114128 | tf_op jit(solution)/shard_map/reduce_scatter | solution.py:746
  673.0 26.4 %swap_blocks.14 = bf16[4,64,2176]{2,1,0:T(8,128)(2,1)} custom-call(bf16[4,64,2176]{2,1,0:T(8,128)(2,1)} %bitcast.234), custom_call_target="tpu_custom_call" | custom-call | flops 15000000512 | bytes 2228224 | tf_op jit(solution)/shard_map/swap_blocks/pallas_call | solution.py:495
  708.7 84.0 %reduce-scatter.5.cloned.1.call-done = bf16[256,4224]{1,0:T(8,128)(2,1)} async-done(((bf16[2048,4224]{1,0:T(8,128)(2,1)}), bf16[256,4224]{1,0:T(8,128)(2,1)}) %reduce-scatter.5.cloned.1.call-update) | async-done | bytes 2162704 | tf_op jit(solution)/shard_map/reduce_scatter | solution.py:668
  792.7 50.3 %swap_blocks.15 = bf16[4,64,4224]{2,1,0:T(8,128)(2,1)} custom-call(bf16[4,64,4224]{2,1,0:T(8,128)(2,1)} %bitcast.279), custom_call_target="tpu_custom_call" | custom-call | flops 15000000512 | bytes 4325376 | tf_op jit(solution)/shard_map/swap_blocks/pallas_call | solution.py:495
  (314 shorter events, 148.1 us)
Async XLA Ops:
  7.2 169.6 %all-gather.5.cloned.1.call-start = ((), (), s32[]{:S(2)}) async-start(), calls=%async_computation.2 | async-start | bytes 7667712 | tf_op jit(solution)/shard_map/all_gather | solution.py:567
  40.3 210.6 %all-gather.7.cloned.1.call-start = ((), (), s32[]{:S(2)}) async-start(), calls=%async_computation.3 | async-start | bytes 2359296 | tf_op jit(solution)/shard_map/all_gather | solution.py:567
  98.0 237.1 %all-gather.9.cloned.1.call-start = ((), (), s32[]{:S(2)}) async-start(), calls=%async_computation.4 | async-start | bytes 12976128 | tf_op jit(solution)/shard_map/all_gather | solution.py:567
  100.6 247.1 %all-gather.11.cloned.1.call-start = ((), (), s32[]{:S(2)}) async-start(), calls=%async_computation.5 | async-start | bytes 6488064 | tf_op jit(solution)/shard_map/all_gather | solution.py:567
  102.8 567.9 %reduce-scatter.3.cloned.1.call-start = ((), (), s32[]{:S(2)}) async-start(), calls=%async_computation.6 | async-start | bytes 10027008 | tf_op jit(solution)/shard_map/reduce_scatter | solution.py:746
  103.1 121.7 %copy-start.8 = (f32[1024]{0:T(1024)}, f32[1024]{0:T(1024)S(1)}, u32[]{:S(2)}) copy-start(f32[1024]{0:T(1024)S(1)} %convert_element_type.171) | copy-start | bytes 12292
  142.8 35.3 %copy-start.59 = (f32[512]{0:T(512)}, f32[512]{0:T(512)S(1)}, u32[]{:S(2)}) copy-start(f32[512]{0:T(512)S(1)} %add_rsqrt_fusion.1) | copy-start | bytes 6148
  142.8 35.3 %copy-start.29 = (bf16[512,2048]{1,0:T(8,128)(2,1)S(1)}, bf16[512,2048]{1,0:T(8,128)(2,1)}, u32[]{:S(2)}) copy-start(bf16[512,2048]{1,0:T(8,128)(2,1)} %gather_line.4) | copy-start | bytes 6291460
  178.1 224.5 %copy-start.44 = (f32[2048,1]{0,1:T(1,128)}, f32[2048,1]{0,1:T(1,128)S(1)}, u32[]{:S(2)}) copy-start(f32[2048,1]{0,1:T(1,128)S(1)} %get-tuple-element.161) | copy-start | bytes 24580
  254.0 42.5 %copy-start.23 = (bf16[128,2048]{1,0:T(8,128)(2,1)S(1)}, bf16[128,2048]{1,0:T(8,128)(2,1)}, u32[]{:S(2)}) copy-start(bf16[128,2048]{1,0:T(8,128)(2,1)} %copy.367.x_ref) | copy-start | bytes 1572868
  296.8 38.3 %copy-start.18 = (f32[128,2048]{1,0:T(8,128)}, f32[128,2048]{1,0:T(8,128)S(1)}, u32[]{:S(2)}) copy-start(f32[128,2048]{1,0:T(8,128)S(1)} %get-tuple-element.140) | copy-start | bytes 3145732
  296.8 105.8 %copy-start.54 = (f32[128]{0:T(128)}, f32[128]{0:T(128)S(1)}, u32[]{:S(2)}) copy-start(f32[128]{0:T(128)S(1)} %add_rsqrt_fusion.3) | copy-start | bytes 1540
  363.0 39.2 %copy-start.19 = (f32[128,2048]{1,0:T(8,128)S(1)}, f32[128,2048]{1,0:T(8,128)}, u32[]{:S(2)}) copy-start(f32[128,2048]{1,0:T(8,128)} %copy-done.18) | copy-start | bytes 3145732
  363.0 40.2 %copy-start.26 = (bf16[128,2048]{1,0:T(8,128)(2,1)S(1)}, bf16[128,2048]{1,0:T(8,128)(2,1)}, u32[]{:S(2)}) copy-start(bf16[128,2048]{1,0:T(8,128)(2,1)} %copy.394.x_ref) | copy-start | bytes 1572868
  535.8 39.6 %copy-start.24 = (bf16[128,2048]{1,0:T(8,128)(2,1)S(1)}, bf16[128,2048]{1,0:T(8,128)(2,1)}, u32[]{:S(2)}) copy-start(bf16[128,2048]{1,0:T(8,128)(2,1)} %copy.367.x_ref) | copy-start | bytes 1572868
  535.8 39.6 %copy-start.56 = (f32[128]{0:T(128)S(1)}, f32[128]{0:T(128)}, u32[]{:S(2)}) copy-start(f32[128]{0:T(128)} %add_rsqrt_fusion.2) | copy-start | bytes 1540
  535.8 40.0 %slice-start = ((bf16[2048,1664]{0,1:T(8,128)(2,1)}), bf16[2048,16]{0,1:T(8,128)(2,1)S(1)}, s32[]{:S(2)}) async-start(bf16[2048,1664]{0,1:T(8,128)(2,1)} %copy-done.25), calls=%async_computation.8 | async-start | bytes 131072 | tf_op jit(solution)/shard_map/slice | solution.py:736
  583.6 209.2 %reduce-scatter.5.cloned.1.call-start = ((), (), s32[]{:S(2)}) async-start(), calls=%async_computation.7 | async-start | bytes 19464192 | tf_op jit(solution)/shard_map/reduce_scatter | solution.py:668
  613.6 39.6 %copy-start.1 = (f32[128,2048]{1,0:T(8,128)S(1)}, f32[128,2048]{1,0:T(8,128)}, u32[]{:S(2)}) copy-start(f32[128,2048]{1,0:T(8,128)} %copy-done) | copy-start | bytes 3145732
  613.6 39.6 %copy-start.20 = (f32[128,2048]{1,0:T(8,128)S(1)}, f32[128,2048]{1,0:T(8,128)}, u32[]{:S(2)}) copy-start(f32[128,2048]{1,0:T(8,128)} %copy-done.18) | copy-start | bytes 3145732
  613.6 39.6 %copy-start.27 = (bf16[128,2048]{1,0:T(8,128)(2,1)S(1)}, bf16[128,2048]{1,0:T(8,128)(2,1)}, u32[]{:S(2)}) copy-start(bf16[128,2048]{1,0:T(8,128)(2,1)} %copy.394.x_ref) | copy-start | bytes 1572868
  613.6 39.6 %copy-start.45 = (f32[2048,1]{0,1:T(1,128)S(1)}, f32[2048,1]{0,1:T(1,128)}, u32[]{:S(2)}) copy-start(f32[2048,1]{0,1:T(1,128)} %copy-done.44) | copy-start | bytes 24580
  613.6 39.6 %copy-start.55 = (f32[128]{0:T(128)S(1)}, f32[128]{0:T(128)}, u32[]{:S(2)}) copy-start(f32[128]{0:T(128)} %copy-done.54) | copy-start | bytes 1540
  613.6 39.6 %copy-start.58 = (f32[128]{0:T(128)S(1)}, f32[128]{0:T(128)}, u32[]{:S(2)}) copy-start(f32[128]{0:T(128)} %copy-done.57) | copy-start | bytes 1540
  (53 other events, 429.7 us)
Sparse Core Ops, SparseCore 0:
  40.4 50.2 all-gather.4
  98.1 29.8 all-gather.6
  130.5 68.7 all-gather.8
  201.6 52.2 all-gather.10
  583.7 86.9 reduce-scatter.2
  674.2 118.5 reduce-scatter.4

commit v2 on v1

--- a/solution.py
+++ b/solution.py
@@ -16,7 +16,8 @@
 CHUNK = 128
 LEVELS = 7
 SMALL = 128
-WAIT_FLOPS = 30_000_000_000
+WAIT_FLOPS = 100_000_000
+PIECES = 2
 norm_eps = 1e-06
 head_eps = 0.25
 decay_norm = 16.0
@@ -265,249 +266,476 @@
     )
 
 
-def greet_line(axis, count):
+def greet(peers):
+    barrier = pltpu.get_barrier_semaphore()
+    number = 0
+    for present, peer in peers:
+        if present is True:
+            pl.semaphore_signal(
+                barrier, inc=1, device_id=peer, device_id_type=pl.DeviceIdType.MESH
+            )
+            number = number + 1
+        else:
+
+            @pl.when(present)
+            def _():
+                pl.semaphore_signal(
+                    barrier, inc=1, device_id=peer, device_id_type=pl.DeviceIdType.MESH
+                )
+
+            number = number + jnp.where(present, 1, 0)
+    pl.semaphore_wait(barrier, number)
+
+
+def line_peers(axis, count):
     me = lax.axis_index(axis)
-    barrier = pltpu.get_barrier_semaphore()
-
-    @pl.when(me > 0)
-    def _():
-        pl.semaphore_signal(
-            barrier, inc=1, device_id={axis: me - 1}, device_id_type=pl.DeviceIdType.MESH
-        )
-
-    @pl.when(me < count - 1)
-    def _():
-        pl.semaphore_signal(
-            barrier, inc=1, device_id={axis: me + 1}, device_id_type=pl.DeviceIdType.MESH
-        )
-
-    pl.semaphore_wait(barrier, jnp.where((me > 0) & (me < count - 1), 2, 1))
-
-
-def gather_body(axis, count, x_ref, out_ref, send, arrive, local_sem):
+    return [(me > 0, {axis: me - 1}), (me < count - 1, {axis: me + 1})]
+
+
+def all_peers(axis, count):
     me = lax.axis_index(axis)
-    own = x_ref.shape[0]
-    greet_line(axis, count)
-
-    def block(index):
-        return out_ref.at[pl.ds(pl.multiple_of(index * own, own), own)]
-
-    def hop(direction, step):
-        index = me - step if direction == 0 else me + step
-        source = x_ref if step == 0 else block(index)
+    return [(True, {axis: lax.rem(me + away, count)}) for away in range(1, count)]
+
+
+class Gather:
+    def __init__(self, axis, count, x_ref, out_ref, send, arrive, local_sem):
+        self.axis, self.count, self.x_ref, self.out_ref = axis, count, x_ref, out_ref
+        self.send, self.arrive = send, arrive
+        self.me = lax.axis_index(axis)
+        self.mine = pltpu.make_async_copy(x_ref, self.block(self.me), local_sem)
+
+    def block(self, index):
+        own = self.x_ref.shape[0]
+        return self.out_ref.at[pl.ds(pl.multiple_of(index * own, own), own)]
+
+    def copy(self, direction, step, index, source):
         return remote(
-            source, block(index), send.at[direction, step], arrive.at[direction, step],
-            axis, me + 1 if direction == 0 else me - 1,
-        )
-
-    def landed(direction, step):
-        index = me - 1 - step if direction == 0 else me + 1 + step
-        return remote(
-            block(index), block(index), send.at[direction, step], arrive.at[direction, step],
-            axis, me + 1 if direction == 0 else me - 1,
-        )
-
-    mine = pltpu.make_async_copy(x_ref, block(me), local_sem)
-    mine.start()
-    for step in range(count):
-        if step > 0:
-
-            @pl.when(me - step >= 0)
-            def _():
-                landed(0, step - 1).wait_recv()
-
-        if step < count - 1:
-
-            @pl.when((me - step >= 0) & (me < count - 1))
-            def _():
-                hop(0, step).start()
-
-        if step > 0:
-
-            @pl.when(me + step <= count - 1)
-            def _():
-                landed(1, step - 1).wait_recv()
-
-        if step < count - 1:
-
-            @pl.when((me + step <= count - 1) & (me > 0))
-            def _():
-                hop(1, step).start()
-
-    for step in range(count - 1):
-
-        @pl.when((me - step >= 0) & (me < count - 1))
-        def _():
-            hop(0, step).wait_send()
-
-        @pl.when((me + step <= count - 1) & (me > 0))
-        def _():
-            hop(1, step).wait_send()
-
-    mine.wait()
-
-
-def gather_line(block, axis, number):
-    count = lax.axis_size(axis)
-    rows, columns = block.shape
-    return pl.pallas_call(
-        functools.partial(gather_body, axis, count),
-        in_specs=[pl.BlockSpec(memory_space=pl.ANY)],
-        out_specs=pl.BlockSpec(memory_space=pl.ANY),
-        out_shape=jax.ShapeDtypeStruct((count * rows, columns), block.dtype),
-        scratch_shapes=[
+            source, self.block(index), self.send.at[direction, step],
+            self.arrive.at[direction, step], self.axis,
+            self.me + 1 if direction == 0 else self.me - 1,
+        )
+
+    def hop(self, direction, step):
+        index = self.me - step if direction == 0 else self.me + step
+        return self.copy(direction, step, index, self.x_ref if step == 0 else self.block(index))
+
+    def landed(self, direction, step):
+        index = self.me - 1 - step if direction == 0 else self.me + 1 + step
+        return self.copy(direction, step, index, self.block(index))
+
+    def holds(self, direction, step):
+        return self.me - step >= 0 if direction == 0 else self.me + step <= self.count - 1
+
+    def hands_on(self, direction, step):
+        inner = self.me < self.count - 1 if direction == 0 else self.me > 0
+        return self.holds(direction, step) & inner
+
+    def start(self):
+        self.mine.start()
+        self.run(0)
+
+    def run(self, first, last=None):
+        for step in range(first, first + 1 if last is None else last):
+            for direction in (0, 1):
+                if step > 0:
+
+                    @pl.when(self.holds(direction, step))
+                    def _():
+                        self.landed(direction, step - 1).wait_recv()
+
+                if step < self.count - 1:
+
+                    @pl.when(self.hands_on(direction, step))
+                    def _():
+                        self.hop(direction, step).start()
+
+    def finish(self):
+        for step in range(self.count - 1):
+            for direction in (0, 1):
+
+                @pl.when(self.hands_on(direction, step))
+                def _():
+                    self.hop(direction, step).wait_send()
+
+        self.mine.wait()
+
+    @staticmethod
+    def scratch(count):
+        return [
             pltpu.SemaphoreType.DMA((2, count - 1)),
             pltpu.SemaphoreType.DMA((2, count - 1)),
             pltpu.SemaphoreType.DMA,
-        ],
-        compiler_params=pltpu.CompilerParams(collective_id=number, has_side_effects=True),
-        cost_estimate=pl.CostEstimate(
-            flops=WAIT_FLOPS, bytes_accessed=count * rows * columns * 4, transcendentals=0
-        ),
-        name="gather_line",
-    )(block)
-
-
-def scatter_body(axis, count, x_ref, out_ref, up, down, send, arrive):
-    me = lax.axis_index(axis)
-    own = out_ref.shape[0]
-    greet_line(axis, count)
-
-    def part(index):
-        return x_ref.at[pl.ds(pl.multiple_of(index * own, own), own)]
-
-    def hop(direction, number, source):
-        held = (up, down)[direction].at[number]
+        ]
+
+
+class Swap:
+    def __init__(self, axis, count, x_ref, out_ref, send, arrive, local_sem):
+        self.axis, self.count, self.x_ref, self.out_ref = axis, count, x_ref, out_ref
+        self.send, self.arrive = send, arrive
+        self.me = lax.axis_index(axis)
+        self.mine = pltpu.make_async_copy(x_ref.at[self.me], out_ref.at[self.me], local_sem)
+
+    def hop(self, away):
+        peer = lax.rem(self.me + away, self.count)
         return remote(
-            source, held, send.at[direction, number], arrive.at[direction, number],
-            axis, me + 1 if direction == 0 else me - 1,
-        )
-
-    def stage(direction, number):
-        target = count - 1 - number if direction == 0 else number
-        first = me == 0 if direction == 0 else me == count - 1
-        passed = me < target if direction == 0 else me > target
-        held = (up, down)[direction].at[number]
-
-        @pl.when(first)
-        def _():
-            hop(direction, number, part(target)).start()
-
-        @pl.when(jnp.logical_not(first) & (passed | (me == target)))
-        def _():
-            hop(direction, number, held).wait_recv()
-
-        @pl.when(jnp.logical_not(first) & passed)
-        def _():
-            held[...] = (held[...].astype(F32) + part(target)[...].astype(F32)).astype(BF)
-            hop(direction, number, held).start()
-
-    for order in (0, 1):
-
-        @pl.when((me >= count // 2) == (order == 1))
-        def _():
-            for number in range(count - 1):
-                stage(order, number)
-                stage(1 - order, number)
-
-    out_ref[...] = part(me)[...].astype(F32)
-    for number in range(count - 1):
-
-        @pl.when(me == count - 1 - number)
-        def _():
-            out_ref[...] += up[number].astype(F32)
-
-        @pl.when(me == number)
-        def _():
-            out_ref[...] += down[number].astype(F32)
-
-    for number in range(count - 1):
-
-        @pl.when(me < count - 1 - number)
-        def _():
-            hop(0, number, up.at[number]).wait_send()
-
-        @pl.when(me > number)
-        def _():
-            hop(1, number, down.at[number]).wait_send()
-
-
-def scatter_line(partial, axis, number):
-    count = lax.axis_size(axis)
-    rows, columns = partial.shape
-    own = rows // count
-    return pl.pallas_call(
-        functools.partial(scatter_body, axis, count),
-        in_specs=[pl.BlockSpec(memory_space=pltpu.VMEM)],
-        out_specs=pl.BlockSpec(memory_space=pltpu.VMEM),
-        out_shape=jax.ShapeDtypeStruct((own, columns), F32),
-        scratch_shapes=[
-            pltpu.VMEM((count - 1, own, columns), BF),
-            pltpu.VMEM((count - 1, own, columns), BF),
-            pltpu.SemaphoreType.DMA((2, count - 1)),
-            pltpu.SemaphoreType.DMA((2, count - 1)),
-        ],
-        compiler_params=pltpu.CompilerParams(
-            collective_id=number, has_side_effects=True, vmem_limit_bytes=32 * 1024 * 1024
-        ),
-        cost_estimate=pl.CostEstimate(
-            flops=WAIT_FLOPS, bytes_accessed=rows * columns * 4, transcendentals=0
-        ),
-        name="scatter_line",
-    )(partial)
-
-
-def swap_body(axis, count, x_ref, out_ref, send, arrive, local_sem):
-    me = lax.axis_index(axis)
-    barrier = pltpu.get_barrier_semaphore()
-    for away in range(1, count):
-        pl.semaphore_signal(
-            barrier, inc=1, device_id={axis: lax.rem(me + away, count)},
-            device_id_type=pl.DeviceIdType.MESH,
-        )
-    pl.semaphore_wait(barrier, count - 1)
-    mine = pltpu.make_async_copy(x_ref.at[me], out_ref.at[me], local_sem)
-    mine.start()
-
-    def hop(away):
-        peer = lax.rem(me + away, count)
+            self.x_ref.at[peer], self.out_ref.at[self.me], self.send.at[away - 1],
+            self.arrive.at[away - 1], self.axis, peer,
+        )
+
+    def landed(self, away):
+        peer = lax.rem(self.me + self.count - away, self.count)
         return remote(
-            x_ref.at[peer], out_ref.at[me], send.at[away - 1], arrive.at[away - 1], axis, peer
-        )
-
-    def landed(away):
-        peer = lax.rem(me + count - away, count)
-        return remote(
-            x_ref.at[peer], out_ref.at[peer], send.at[away - 1], arrive.at[away - 1], axis, peer
-        )
-
-    for away in range(1, count):
-        hop(away).start()
-    for away in range(1, count):
-        landed(away).wait_recv()
-    for away in range(1, count):
-        hop(away).wait_send()
-    mine.wait()
-
-
-def swap_blocks(value, axis, number):
-    count = lax.axis_size(axis)
-    return pl.pallas_call(
-        functools.partial(swap_body, axis, count),
-        in_specs=[pl.BlockSpec(memory_space=pl.ANY)],
-        out_specs=pl.BlockSpec(memory_space=pl.ANY),
-        out_shape=jax.ShapeDtypeStruct(value.shape, value.dtype),
-        scratch_shapes=[
+            self.x_ref.at[peer], self.out_ref.at[peer], self.send.at[away - 1],
+            self.arrive.at[away - 1], self.axis, peer,
+        )
+
+    def start(self):
+        self.mine.start()
+        for away in range(1, self.count):
+            self.hop(away).start()
+
+    def finish(self):
+        for away in range(1, self.count):
+            self.landed(away).wait_recv()
+        for away in range(1, self.count):
+            self.hop(away).wait_send()
+        self.mine.wait()
+
+    @staticmethod
+    def scratch(count):
+        return [
             pltpu.SemaphoreType.DMA((count - 1,)),
             pltpu.SemaphoreType.DMA((count - 1,)),
             pltpu.SemaphoreType.DMA,
+        ]
+
+
+class Scatter:
+    def __init__(self, axis, count, pieces, x_ref, out_ref, up, down, send, arrive):
+        self.axis, self.count, self.pieces = axis, count, pieces
+        self.x_ref, self.out_ref, self.held_refs = x_ref, out_ref, (up, down)
+        self.send, self.arrive = send, arrive
+        self.me = lax.axis_index(axis)
+        self.own = out_ref.shape[0]
+        self.size = self.own // pieces
+
+    def part(self, index, piece):
+        start = pl.multiple_of(index * self.own + piece * self.size, self.size)
+        return self.x_ref.at[pl.ds(start, self.size)]
+
+    def held(self, direction, number, piece):
+        return self.held_refs[direction].at[number, pl.ds(piece * self.size, self.size)]
+
+    def hop(self, direction, number, piece, source=None):
+        held = self.held(direction, number, piece)
+        return remote(
+            held if source is None else source, held, self.send.at[direction, number, piece],
+            self.arrive.at[direction, number, piece], self.axis,
+            self.me + 1 if direction == 0 else self.me - 1,
+        )
+
+    def target(self, direction, number):
+        return self.count - 1 - number if direction == 0 else number
+
+    def start(self):
+        for direction in (0, 1):
+
+            @pl.when(self.me == (0 if direction == 0 else self.count - 1))
+            def _():
+                for number in range(self.count - 1):
+                    target = self.target(direction, number)
+                    for piece in range(self.pieces):
+                        self.hop(direction, number, piece, self.part(target, piece)).start()
+
+    def stage(self, direction, number, piece):
+        me, target = self.me, self.target(direction, number)
+        inner = me > 0 if direction == 0 else me < self.count - 1
+        passed = me < target if direction == 0 else me > target
+        held = self.held(direction, number, piece)
+
+        @pl.when(inner & (passed | (me == target)))
+        def _():
+            self.hop(direction, number, piece).wait_recv()
+
+        @pl.when(inner & passed)
+        def _():
+            mine = self.part(target, piece)[...].astype(F32)
+            held[...] = (held[...].astype(F32) + mine).astype(BF)
+            self.hop(direction, number, piece).start()
+
+    def run(self, number, far):
+        for order in (0, 1):
+
+            @pl.when((self.me >= self.count // 2) == (order == 1))
+            def _():
+                for piece in range(self.pieces):
+                    self.stage(1 - order if far else order, number, piece)
+
+    def finish(self):
+        me, count, out_ref = self.me, self.count, self.out_ref
+        for piece in range(self.pieces):
+            rows = pl.ds(piece * self.size, self.size)
+            out_ref[rows] = self.part(me, piece)[...].astype(F32)
+            for direction in (0, 1):
+                for number in range(count - 1):
+                    inner = me > 0 if direction == 0 else me < count - 1
+
+                    @pl.when((me == self.target(direction, number)) & inner)
+                    def _():
+                        out_ref[rows] += self.held(direction, number, piece)[...].astype(F32)
+
+        for direction in (0, 1):
+            for number in range(count - 1):
+                target = self.target(direction, number)
+
+                @pl.when(me < target if direction == 0 else me > target)
+                def _():
+                    for piece in range(self.pieces):
+                        self.hop(direction, number, piece).wait_send()
+
+    @staticmethod
+    def scratch(count, own, columns, pieces):
+        return [
+            pltpu.VMEM((count - 1, own, columns), BF),
+            pltpu.VMEM((count - 1, own, columns), BF),
+            pltpu.SemaphoreType.DMA((2, count - 1, pieces)),
+            pltpu.SemaphoreType.DMA((2, count - 1, pieces)),
+        ]
+
+
+class Spread:
+    def __init__(self, sizes, x_ref, out_ref, send, arrive, far_send, far_arrive, near_send,
+                 near_arrive, local_sem):
+        self.X, self.C, self.Z, self.Y = sizes
+        self.x_ref, self.out_ref = x_ref, out_ref
+        self.send, self.arrive = send, arrive
+        self.far_send, self.far_arrive = far_send, far_arrive
+        self.near_send, self.near_arrive = near_send, near_arrive
+        self.x, self.c, self.z, self.y = (lax.axis_index(name) for name in OWN)
+        self.others = self.X * self.Y - 1
+        self.mine = pltpu.make_async_copy(
+            x_ref.at[self.z], self.place(0, self.c, 0), local_sem
+        )
+
+    def across(self, offset, sign):
+        down, right = offset // self.Y, offset % self.Y
+        if sign < 0:
+            down, right = self.X - down, self.Y - right
+        return lax.rem(self.x + down, self.X), lax.rem(self.y + right, self.Y)
+
+    def place(self, offset, c, slot):
+        x, y = self.across(offset, -1)
+        z = lax.rem(self.z + self.Z - slot, self.Z)
+        return self.out_ref.at[((x * self.C + c) * self.Y + y) * self.Z + z]
+
+    def along(self, away):
+        return remote(
+            self.x_ref.at[lax.rem(self.z + away, self.Z)], self.place(0, self.c, 0),
+            self.send.at[away - 1], self.arrive.at[away - 1], "z",
+            lax.rem(self.z + away, self.Z),
+        )
+
+    def along_landed(self, away):
+        held = self.place(0, self.c, away)
+        return remote(
+            held, held, self.send.at[away - 1], self.arrive.at[away - 1], "z",
+            lax.rem(self.z + away, self.Z),
+        )
+
+    def far(self, offset, slot, landed=False):
+        x, y = self.across(offset, 1)
+        held = self.place(offset if landed else 0, self.c, slot)
+        source = self.x_ref.at[self.z] if slot == 0 and not landed else held
+        return pltpu.make_async_remote_copy(
+            src_ref=source, dst_ref=held, send_sem=self.far_send.at[offset - 1, slot],
+            recv_sem=self.far_arrive.at[offset - 1, slot], device_id={"x": x, "y": y},
+            device_id_type=pl.DeviceIdType.MESH,
+        )
+
+    def near(self, offset, slot, landed=False):
+        held = self.place(offset, 1 - self.c if landed else self.c, slot)
+        direct = offset == 0 and slot == 0 and not landed
+        return remote(
+            self.x_ref.at[self.z] if direct else held, held, self.near_send.at[offset, slot],
+            self.near_arrive.at[offset, slot], "c", 1 - self.c,
+        )
+
+    def peers(self):
+        found = all_peers("z", self.Z) + [(True, {"c": 1 - self.c})]
+        for offset in range(1, self.others + 1):
+            x, y = self.across(offset, 1)
+            found.append((True, {"x": x, "y": y}))
+        return found
+
+    def start(self):
+        self.mine.start()
+        for away in range(1, self.Z):
+            self.along(away).start()
+        self.hand_on(0)
+
+    def hand_on(self, slot):
+        if slot > 0:
+            self.along_landed(slot).wait_recv()
+        for offset in range(1, self.others + 1):
+            self.far(offset, slot).start()
+        self.near(0, slot).start()
+
+    def collect(self, slot):
+        for offset in range(1, self.others + 1):
+            self.far(offset, slot, True).wait_recv()
+            self.near(offset, slot).start()
+
+    def finish(self):
+        for slot in range(self.Z):
+            for offset in range(self.others + 1):
+                self.near(offset, slot, True).wait_recv()
+        for slot in range(self.Z):
+            for offset in range(self.others + 1):
+                self.near(offset, slot).wait_send()
+                if offset > 0:
+                    self.far(offset, slot).wait_send()
+        for away in range(1, self.Z):
+            self.along(away).wait_send()
+        self.mine.wait()
+
+    @staticmethod
+    def scratch(sizes):
+        X, C, Z, Y = sizes
+        far = pltpu.SemaphoreType.DMA((max(X * Y - 1, 1), Z))
+        near = pltpu.SemaphoreType.DMA((X * Y, Z))
+        line = pltpu.SemaphoreType.DMA((Z - 1,))
+        return [line, line, far, far, near, near, pltpu.SemaphoreType.DMA]
+
+
+def spread_and_gather(value, block, other, sizes, number):
+    X, C, Z, Y = sizes
+
+    def body(v_ref, x_ref, o_ref, spread_ref, out_ref, swapped_ref, *sems):
+        spread = Spread(sizes, v_ref, spread_ref, *sems[:7])
+        gather = Gather("z", Z, x_ref, out_ref, *sems[7:10])
+        swap = Swap("z", Z, o_ref, swapped_ref, *sems[10:])
+        greet(spread.peers())
+        spread.start()
+        gather.start()
+        for slot in range(1, Z):
+            spread.hand_on(slot)
+        for step in range(1, Z):
+            gather.run(step)
+            if step == Z - 2:
+                swap.start()
+            spread.collect(step - 1)
+        spread.collect(Z - 1)
+        spread.finish()
+        gather.finish()
+        swap.finish()
+
+    anywhere = pl.BlockSpec(memory_space=pl.ANY)
+    return pl.pallas_call(
+        body,
+        in_specs=[anywhere] * 3,
+        out_specs=[anywhere] * 3,
+        out_shape=[
+            jax.ShapeDtypeStruct((X * C * Y * Z,) + value.shape[1:], value.dtype),
+            jax.ShapeDtypeStruct((Z * block.shape[0],) + block.shape[1:], block.dtype),
+            jax.ShapeDtypeStruct(other.shape, other.dtype),
         ],
+        scratch_shapes=Spread.scratch(sizes) + Gather.scratch(Z) + Swap.scratch(Z),
         compiler_params=pltpu.CompilerParams(collective_id=number, has_side_effects=True),
         cost_estimate=pl.CostEstimate(
-            flops=WAIT_FLOPS // 2, bytes_accessed=value.size * 4, transcendentals=0
+            flops=WAIT_FLOPS, bytes_accessed=value.size * X * C * Y * 2, transcendentals=0
         ),
-        name="swap_blocks",
-    )(value)
+        name="spread_and_gather",
+    )(value, block, other)
+
+
+def move(number, scatter=None, swaps=(), gathers=(), extras=(), post=None):
+    in_vmem, anywhere = pl.BlockSpec(memory_space=pltpu.VMEM), pl.BlockSpec(memory_space=pl.ANY)
+    values, in_specs, shapes, out_specs, scratch = [], [], [], [], []
+    flags = {}
+
+    def scale(axis):
+        return lax.axis_size(axis)
+
+    if scatter is not None:
+        partial, axis = scatter
+        own = partial.shape[0] // scale(axis)
+        values += [partial, *extras]
+        in_specs += [in_vmem] * (1 + len(extras))
+        shapes.append(jax.ShapeDtypeStruct((own, partial.shape[1]), F32))
+        out_specs.append(in_vmem)
+        scratch += Scatter.scratch(scale(axis), own, partial.shape[1], PIECES)
+        flags = dict(vmem_limit_bytes=40 * 1024 * 1024)
+    for value, axis in swaps:
+        values.append(value)
+        in_specs.append(anywhere)
+        shapes.append(jax.ShapeDtypeStruct(value.shape, value.dtype))
+        out_specs.append(anywhere)
+        scratch += Swap.scratch(scale(axis))
+    for block, axis in gathers:
+        values.append(block)
+        in_specs.append(anywhere)
+        shapes.append(
+            jax.ShapeDtypeStruct((scale(axis) * block.shape[0], block.shape[1]), block.dtype)
+        )
+        out_specs.append(anywhere)
+        scratch += Gather.scratch(scale(axis))
+
+    def body(*refs):
+        ins = list(refs[: len(values)])
+        outs = list(refs[len(values) : len(values) + len(shapes)])
+        sems = list(refs[len(values) + len(shapes) :])
+        peers = {}
+        adding, extra_refs, swapping, gathering = None, (), [], []
+        if scatter is not None:
+            axis = scatter[1]
+            adding = Scatter(axis, scale(axis), PIECES, ins.pop(0), outs.pop(0), *sems[:4])
+            extra_refs, ins, sems = ins[: len(extras)], ins[len(extras) :], sems[4:]
+            peers[axis] = line_peers(axis, scale(axis))
+        for _, axis in gathers:
+            peers[axis] = line_peers(axis, scale(axis))
+        for _, axis in swaps:
+            peers[axis] = all_peers(axis, scale(axis))
+            swapping.append(Swap(axis, scale(axis), ins.pop(0), outs.pop(0), *sems[:3]))
+            sems = sems[3:]
+        for _, axis in gathers:
+            gathering.append(Gather(axis, scale(axis), ins.pop(0), outs.pop(0), *sems[:3]))
+            sems = sems[3:]
+        greet([peer for found in peers.values() for peer in found])
+        for part in gathering + ([adding] if adding else []) + swapping:
+            part.start()
+        steps = max([part.count for part in gathering + ([adding] if adding else [])] + [0])
+        for part in gathering:
+            part.run(1)
+        for step in range(1, steps):
+            if adding:
+                adding.run(step - 1, False)
+            for part in gathering:
+                if step + 1 < part.count:
+                    part.run(step + 1)
+            if adding:
+                adding.run(step - 1, True)
+        if adding:
+            adding.finish()
+            if post is not None:
+                adding.out_ref[...] = post(adding.out_ref[...], *[r[...] for r in extra_refs])
+        for part in swapping + gathering:
+            part.finish()
+
+    size = sum(v.size for v in values)
+    return pl.pallas_call(
+        body,
+        in_specs=in_specs,
+        out_specs=out_specs,
+        out_shape=shapes,
+        scratch_shapes=scratch,
+        compiler_params=pltpu.CompilerParams(
+            collective_id=number, has_side_effects=True, **flags
+        ),
+        cost_estimate=pl.CostEstimate(
+            flops=WAIT_FLOPS, bytes_accessed=size * 4, transcendentals=0
+        ),
+        name="move",
+    )(*values)
 
 
 def local(
@@ -529,10 +757,14 @@
         cut = value.reshape(lead + (X, C, Z, Y, rows))
         return jnp.swapaxes(cut, -3, -2).reshape(lead + (width,))
 
-    def unblocked(value):
-        lead = value.shape[:-1]
-        cut = value.reshape(lead + (X, C, Y, Z, rows))
-        return jnp.swapaxes(cut, -3, -2).reshape(lead + (width,))
+    def straight(value):
+        found = []
+        for start in range(0, width, Z * Y * rows):
+            for at_z in range(Z):
+                for at_y in range(Y):
+                    first_lane = start + (at_y * Z + at_z) * rows
+                    found.append(value[:, first_lane : first_lane + rows])
+        return jnp.concatenate(found, axis=1)
 
     def cut_columns(weight):
         return jnp.swapaxes(weight.reshape(rows, Z, weight.shape[1] // Z), 0, 1)
@@ -543,17 +775,14 @@
 
     numbers = iter(range(32))
 
-    def swap_z(value):
-        return swap_blocks(value, "z", next(numbers))
-
     def swap_y(value):
-        return swap_blocks(value, "y", next(numbers))
+        return move(next(numbers), swaps=[(value, "y")])[0]
 
     def gather_z(value):
-        return gather_line(value, "z", next(numbers))
-
-    def scatter_z(value):
-        return scatter_line(value.astype(BF), "z", next(numbers))
+        return move(next(numbers), gathers=[(value, "z")])[0]
+
+    def after(value, *others):
+        return lax.optimization_barrier((value,) + others)[0]
 
     def to_sequence(value):
         cut = value.reshape(Y, Z, own, value.shape[-1])
@@ -563,8 +792,12 @@
         cut = value.reshape(Z, Y, own, value.shape[-1])
         return jnp.swapaxes(cut, 0, 1).reshape(Y, group, value.shape[-1])
 
+    def scatter_rest(value):
+        sums = lax.psum_scatter(value, REST, scatter_dimension=0, tiled=True)
+        return sums.reshape(Z, rows, -1)
+
     def gather_rest(value):
-        return lax.all_gather(value, REST, axis=0, tiled=True)
+        return lax.all_gather(value.reshape(Z * rows, -1), REST, axis=0, tiled=True)
 
     small = jnp.concatenate(
         [
@@ -579,22 +812,18 @@
         + [jnp.broadcast_to(small[None], (Z,) + small.shape)],
         axis=2,
     )
-    input_weights = gather_rest(swap_z(first).reshape(Z * rows, -1))
-    second = swap_z(
-        jnp.concatenate(
-            [cut_columns(w) for w in (out_weight, mlp_gate_weight, mlp_up_weight, down_weight)],
-            axis=2,
-        )
-    ).reshape(Z * rows, -1)
-    out_piece = gather_rest(second[:, :DV])
-    mlp_piece = gather_rest(second[:, DV : DV + 2 * ff])
-    down_piece = gather_rest(second[:, DV + 2 * ff :])
-
     own_tokens = blocked(tokens)
-    group_tokens = gather_z(own_tokens)
-    group_cotangent = gather_z(blocked(cotangent))
+    input_weights, group_tokens, out_weights = spread_and_gather(
+        first, own_tokens, cut_columns(out_weight), (X, C, Z, Y), next(numbers)
+    )
+    input_weights = input_weights.reshape(width, -1)
+    mlp_weights = jnp.concatenate(
+        [cut_columns(mlp_gate_weight), cut_columns(mlp_up_weight)], axis=2
+    )
+    down_weights = cut_columns(down_weight)
 
     projected = 2 * DK + 2 * DV
+    near = 2 * DK + DV
     small_all = input_weights[:, projected:].astype(F32)
 
     def device_rows(value, count):
@@ -618,7 +847,10 @@
     shared = jnp.concatenate([low[:, : 2 * DK], low[:, projected:]], axis=1)
     values = jnp.swapaxes(low[:, 2 * DK : 2 * DK + DV].reshape(group, Y, dvp), 0, 1)
     sent = jnp.concatenate([jnp.broadcast_to(shared[None], (Y,) + shared.shape), values], axis=2)
-    sequence = to_sequence(swap_y(sent))
+    sent, mlp_weights = move(next(numbers), swaps=[(sent, "y"), (mlp_weights, "z")])
+    out_piece = gather_rest(out_weights)
+    mlp_piece = gather_rest(mlp_weights)
+    sequence = to_sequence(sent)
     queries = sequence[:, :DK]
     keys = sequence[:, DK : 2 * DK]
     rank_low = sequence[:, 2 * DK : 2 * DK + R]
@@ -639,7 +871,11 @@
     seg_rows = cut.astype(F32)[:, None, :]
 
     mixed_part, enter, scores = mix_forward(queries, keys, value_part, log_decay, aux, seg_rows)
-    mixed = jnp.swapaxes(swap_y(from_sequence(mixed_part)), 0, 1).reshape(group, DV).astype(F32)
+    mixed_part, down_weights = move(
+        next(numbers), swaps=[(from_sequence(mixed_part), "y"), (down_weights, "z")]
+    )
+    down_piece = gather_rest(down_weights)
+    mixed = jnp.swapaxes(mixed_part, 0, 1).reshape(group, DV).astype(F32)
 
     head_scale = lax.rsqrt(jnp.mean(mixed * mixed, axis=1, keepdims=True) + head_eps)
     head_hat = mixed * head_scale
@@ -647,7 +883,12 @@
     sig_out = jax.nn.sigmoid(out_gate)
     silu_out = out_gate * sig_out
     gated = (head_out * silu_out).astype(BF)
-    residual = own_tokens.astype(F32) + scatter_z(dot_rows(gated, out_piece))
+    own_cotangent = blocked(cotangent)
+    residual, group_cotangent = move(
+        next(numbers), scatter=(dot_rows(gated, out_piece).astype(BF), "z"),
+        gathers=[(own_cotangent, "z")], extras=[own_tokens],
+        post=lambda total_sum, x: total_sum + x.astype(F32),
+    )
     scale_mid = lax.rsqrt(jnp.mean(residual * residual, axis=1, keepdims=True) + norm_eps)
     hat_mid = residual * scale_mid
     normed_mlp = gather_z((hat_mid * mlp_gain_all).astype(BF))
@@ -662,23 +903,28 @@
     grad_gate = (grad_hidden * up_pre * sig_gate * (1.0 + gate_pre * (1.0 - sig_gate))).astype(BF)
     grad_up = (grad_hidden * silu_gate).astype(BF)
     grad_both = jnp.concatenate([grad_gate, grad_up], axis=1)
-    grad_normed_mlp = scatter_z(dot_rows(grad_both, mlp_piece))
-    layer_out = residual + scatter_z(dot_rows(hidden, down_piece))
-
-    mlp_sums = lax.psum_scatter(
-        jnp.concatenate(
-            [dot_cols(normed_mlp, grad_both), dot_cols(group_cotangent, hidden)], axis=1
-        ).astype(BF),
-        REST, scatter_dimension=0, tiled=True,
-    )
-    mlp_rows = swap_z(mlp_sums.reshape(Z, rows, 3 * ff)).astype(F32)
+    out_partial = dot_rows(hidden, down_piece).astype(BF)
+    mlp_back, down_partial = lax.optimization_barrier(
+        (
+            dot_rows(grad_both, mlp_piece).astype(BF),
+            dot_cols(group_cotangent, hidden).astype(BF),
+        )
+    )
+    down_sums = scatter_rest(down_partial)
+    grad_normed_mlp = move(next(numbers), scatter=(mlp_back, "z"))[0]
+    mlp_partial = dot_cols(normed_mlp, grad_both).astype(BF)
 
     mlp_gain_part = jnp.sum(grad_normed_mlp * hat_mid, axis=0)
     scaled = grad_normed_mlp * mlp_gain_all
-    grad_residual = blocked(cotangent).astype(F32) + scale_mid * (
+    grad_residual = own_cotangent.astype(F32) + scale_mid * (
         scaled - hat_mid * jnp.mean(scaled * hat_mid, axis=1, keepdims=True)
     )
-    grad_branch = gather_z(grad_residual.astype(BF))
+    branch_own, mlp_partial = lax.optimization_barrier((grad_residual.astype(BF), mlp_partial))
+    mlp_sums = scatter_rest(after(mlp_partial, down_sums))
+    layer_out, grad_branch = move(
+        next(numbers), scatter=(out_partial, "z"), gathers=[(branch_own, "z")],
+        extras=[residual], post=lambda total_sum, rest: straight(total_sum + rest),
+    )
     grad_gated = dot_plain(grad_branch, out_piece)
     grad_head = grad_gated * silu_out
     head_gain_part = jnp.sum(grad_head * head_hat, axis=0)
@@ -694,7 +940,15 @@
         queries, keys, value_part, log_decay, aux, seg_rows, enter, scores, grad_part
     )
     dlogit = (dld * jax.nn.sigmoid(-decay_logit) / decay_norm).astype(BF)
-    back = swap_y(from_sequence(jnp.concatenate([dq, dk, dlogit, dv], axis=1)))
+    back = from_sequence(jnp.concatenate([dq, dk, dlogit, dv], axis=1))
+    side_partial = jnp.concatenate(
+        [dot_cols(normed_in, grad_out_gate), dot_cols(grad_branch, gated)], axis=1
+    ).astype(BF)
+    back, side_partial = lax.optimization_barrier((back, side_partial))
+    side_sums = scatter_rest(after(side_partial, mlp_sums))
+    back, down_rows, mlp_rows = move(
+        next(numbers), swaps=[(back, "y"), (down_sums, "z"), (mlp_sums, "z")]
+    )
     summed = jnp.sum(back[:, :, : 3 * DK].astype(F32), axis=0).astype(BF)
     grad_value = jnp.swapaxes(back[:, :, 3 * DK :], 0, 1).reshape(group, DV)
     grad_logit = summed[:, 2 * DK :]
@@ -709,16 +963,8 @@
         ],
         axis=1,
     )
-    grad_normed_in = scatter_z(dot_rows(grad_heads, input_weights))
-    rows_own = own_tokens.astype(F32)
-    scale_own = lax.rsqrt(jnp.mean(rows_own * rows_own, axis=1, keepdims=True) + norm_eps)
-    hat_own = rows_own * scale_own
-    attn_gain_part = jnp.sum(grad_normed_in * hat_own, axis=0)
-    scaled_in = grad_normed_in * attn_gain_all
-    tokens_grad = grad_residual + scale_own * (
-        scaled_in - hat_own * jnp.mean(scaled_in * hat_own, axis=1, keepdims=True)
-    )
-
+    normed_in_partial = dot_rows(grad_heads, input_weights)
+    attn_gain_part = jnp.sum(normed_in_partial * (rows_in * scale_in), axis=0)
     def to_device_rows(value, count):
         cut = value.reshape(X, C, Z, Y, rows // count, -1)
         cut = jnp.swapaxes(cut, 2, 3)
@@ -730,10 +976,12 @@
             jnp.zeros((H * DK, value.shape[1]), F32), value, z * DK, 0
         )
 
-    weight_part = dot_cols(normed_in, grad_heads)
+    near_part = dot_cols(
+        normed_in, jnp.concatenate([grad_heads[:, :near], grad_heads[:, projected:]], axis=1)
+    )
     small_part = jnp.concatenate(
         [
-            weight_part[:, projected : projected + R],
+            near_part[:, near : near + R],
             attn_gain_part[:, None],
             mlp_gain_part[:, None],
             to_device_rows(at_head(rank_out_part), width // (H * DK)),
@@ -743,35 +991,47 @@
         axis=1,
     )
     small_part = jnp.pad(small_part, ((0, 0), (0, SMALL - small_part.shape[1])))
-    attn_sums = lax.psum_scatter(
-        jnp.concatenate(
-            [weight_part[:, :projected], dot_cols(grad_branch, gated), small_part], axis=1
-        ).astype(BF),
-        REST, scatter_dimension=0, tiled=True,
-    )
-    attn_rows = swap_z(attn_sums.reshape(Z, rows, -1)).astype(F32)
+    near_partial = jnp.concatenate([near_part[:, :near], small_part], axis=1).astype(BF)
+    partial, near_partial = lax.optimization_barrier(
+        (normed_in_partial.astype(BF), near_partial)
+    )
+    near_sums = scatter_rest(after(near_partial, side_sums))
+
+    def finish_tokens(back_sum, x, grad_res, gain):
+        held = x.astype(F32)
+        scale = lax.rsqrt(jnp.mean(held * held, axis=1, keepdims=True) + norm_eps)
+        hat = held * scale
+        scaled = back_sum * gain
+        mean = jnp.mean(scaled * hat, axis=1, keepdims=True)
+        return straight(grad_res + scale * (scaled - hat * mean))
+
+    tokens_grad, side_rows = move(
+        next(numbers), scatter=(partial, "z"), swaps=[(side_sums, "z")],
+        extras=[own_tokens, grad_residual, attn_gain_all[None]], post=finish_tokens,
+    )
+    near_rows = move(next(numbers), swaps=[(after(near_sums, tokens_grad), "z")])[0]
 
     def joined(value):
-        return jnp.swapaxes(value, 0, 1).reshape(rows, -1)
-
-    small_rows = jnp.sum(attn_rows[:, :, projected + DV :], axis=0)
+        return jnp.swapaxes(value, 0, 1).reshape(rows, -1).astype(F32)
+
+    small_rows = jnp.sum(near_rows[:, :, near : near + SMALL].astype(F32), axis=0)
     return (
-        unblocked(layer_out),
-        unblocked(tokens_grad),
+        layer_out,
+        tokens_grad,
         small_rows[:, R],
-        joined(attn_rows[:, :, :DK]),
-        joined(attn_rows[:, :, DK : 2 * DK]),
-        joined(attn_rows[:, :, 2 * DK : 2 * DK + DV]),
-        joined(attn_rows[:, :, 2 * DK + DV : projected]),
+        joined(near_rows[:, :, :DK]),
+        joined(near_rows[:, :, DK : 2 * DK]),
+        joined(near_rows[:, :, 2 * DK : near]),
+        joined(side_rows[:, :, :DV]),
         small_rows[:, :R],
         small_rows[: rows * H * DK // width, R + 2 : 2 * R + 2],
         small_rows[: rows * H * DK // width, 2 * R + 2],
         small_rows[: rows * DV // width, 2 * R + 3],
-        joined(attn_rows[:, :, projected : projected + DV]),
+        joined(side_rows[:, :, DV:]),
         small_rows[:, R + 1],
         joined(mlp_rows[:, :, :ff]),
-        joined(mlp_rows[:, :, ff : 2 * ff]),
-        joined(mlp_rows[:, :, 2 * ff :]),
+        joined(mlp_rows[:, :, ff:]),
+        joined(down_rows),
     )
 
 

time: 860 us -> 659 us (0.77)
  Pallas kernels: 559 us -> 427 us
  waiting for transfers between devices: 94.9 us -> 22.2 us
  other arithmetic: 39.1 us -> 25.6 us
  starting transfers between devices: 0.25 us -> 12.8 us
    pallas_call x16 -> x11, Pallas kernels: 537 us -> 405 us  [the longest x10 345 us: move(): pl.pallas_call(body, in_specs=in_specs, out_specs=out_specs, out_shape=sh...]
    reduce_scatter x2 -> x4, waiting for transfers between devices: 94.8 us -> 22 us  [scatter_rest(): sums = lax.psum_scatter(value, REST, scatter_dimension=0, tiled=True)]
    reduce_scatter x2 -> x4, starting transfers between devices: 0.08 us -> 12.7 us  [scatter_rest(): sums = lax.psum_scatter(value, REST, scatter_dimension=0, tiled=True)]
    reshape x9 -> x0, local copies, waits for them, and re-layouts: 9.94 us -> none  [the longest x8 7.61 us: joined(): return jnp.swapaxes(value, 0, 1).reshape(rows, -1)]
    unnamed x159 -> x145, local copies, waits for them, and re-layouts: 16.2 us -> 24.6 us
    dot_general x5 -> x6, matrix products: 24.7 us -> 22.7 us  [dot_cols(): lax.dot_general(left, right, (((0,), (0,)), ((), ())), preferred_element_...]
  transfers between devices with their start and end apart: 6 -> 7, of which waited for: 2 -> 2; matrix products, arithmetic and copies ran while one was open for 12% -> 17% of each run, Pallas kernels for 37% -> 53%
where the time goes in v2:
time: 659 us; the launch traced here: 657 us
  Pallas kernels  427 us (65%)
  matrix products  89.1 us (14%)
  local copies, waits for them, and re-layouts  64.9 us (10%)
  other arithmetic  25.6 us (4%)
  waiting for transfers between devices  22.2 us (3%)
  between operations  15.5 us (2%)
  starting transfers between devices  12.8 us (2%)
    pallas_call x10, Pallas kernels, move(): pl.pallas_call(body, in_specs=in_specs, out_specs=out_specs, out_shape=sh...  345 us
    pallas_call x1, Pallas kernels, spread_and_gather(): pl.pallas_call(body, in_specs=[anywhere] * 3, out_specs=[anywhere] * 3, o...  60.5 us
    dot_general x5, matrix products, dot_plain(): return jnp.dot(left, right, preferred_element_type=F32)  34.6 us
    dot_general x5, matrix products, dot_rows(): lax.dot_general(left, right, (((1,), (1,)), ((), ())), preferred_element_...  31.7 us
    unnamed x145, local copies, waits for them, and re-layouts  24.6 us
    dot_general x6, matrix products, dot_cols(): lax.dot_general(left, right, (((0,), (0,)), ((), ())), preferred_element_...  22.7 us
    reduce_scatter x4, waiting for transfers between devices, scatter_rest(): sums = lax.psum_scatter(value, REST, scatter_dimension=0, tiled=True)  22 us
    pallas_call x1, Pallas kernels, mix_backward(): pl.pallas_call(mix_backward_body, grid=(count,), in_specs=[tokens(DK), to...  13.9 us
  transfers between devices with their start and end apart: 7, of which 2 were waited for; matrix products, arithmetic and copies ran while one was open for 17% of the time, Pallas kernels for 53%

profile of v2, /device:TPU:9, one launch (start us, length us, event | category | flops | bytes accessed | tf_op | source)
XLA Modules:
  0.0 657.2 jit_solution(1146302507747559035)
XLA Ops:
  16.0 60.5 %spread_and_gather.1 = (bf16[32,64,1664]{2,1,0:T(8,128)(2,1)}, bf16[512,2048]{1,0:T(8,128)(2,1)}, bf16[4,64,512]{2,1,0:T(8,128)(2,1)}) custom-call(bf16[4,64,1664]{2,1,0:T(8,128)(2,1)} %copy-done.38, bf16[128,2048]{1,0:T(8,128)(2,1)} %copy.345.x_ref.refs_1_, bf16[4,64,512]{2,1,0:T(8,128)(2,1)} %bitcast.228), custom_call_target="tpu_custom_call" | custom-call | flops 100000000 | bytes 6815744 | tf_op jit(solution)/shard_map/spread_and_gather/pallas_call | solution.py:633
  78.8 8.7 %fusion.49 = (bf16[512,1664]{1,0:T(8,128)(2,1)S(1)}, f32[512,1664]{1,0:T(8,128)}) fusion(bf16[2048,1664]{1,0:T(8,128)(2,1)} %bitcast.257, bf16[512,2048]{1,0:T(8,128)(2,1)S(1)} %copy-done.33, f32[2048]{0:T(1024)S(1)} %bitcast.264, f32[512]{0:T(512)S(1)} %add_rsqrt_fusion.1), kind=kOutput, calls=%fused_computation.133 | convolution fusion | flops 3494707200 | bytes 14034944 | tf_op jit(solution)/shard_map/dot_general | solution.py:31
  92.3 45.8 %move.10 = (bf16[2,512,896]{2,1,0:T(8,128)(2,1)}, bf16[4,64,2816]{2,1,0:T(8,128)(2,1)}) custom-call(bf16[2,512,896]{2,1,0:T(8,128)(2,1)} %pad_maximum_fusion.5.refs_0_, bf16[4,64,2816]{2,1,0:T(8,128)(2,1)} %pad_maximum_fusion.6.refs_1_), custom_call_target="tpu_custom_call" | custom-call | flops 100000000 | bytes 6553600 | tf_op jit(solution)/shard_map/move/pallas_call | solution.py:725
  145.2 7.9 %mix_forward.1 = (bf16[1024,256]{1,0:T(8,128)(2,1)S(1)}, bf16[8,256,256]{2,1,0:T(8,128)(2,1)S(1)}, bf16[8,128,128]{2,1,0:T(8,128)(2,1)S(1)}) custom-call(bf16[1024,256]{1,0:T(8,128)(2,1)S(1)} %get-tuple-element.172.q_ref, bf16[1024,256]{1,0:T(8,128)(2,1)S(1)} %get-tuple-element.171.k_ref, bf16[1024,256]{1,0:T(8,128)(2,1)S(1)} %get-tuple-element.170.v_ref, ...), custom_call_target="tpu_custom_call" | custom-call | flops 2080374784 | bytes 4194304 | tf_op jit(solution)/shard_map/mix_forward/pallas_call | solution.py:200
  155.2 18.7 %move.11 = (bf16[2,512,256]{2,1,0:T(8,128)(2,1)}, bf16[4,64,1408]{2,1,0:T(8,128)(2,1)}) custom-call(bf16[2,512,256]{2,1,0:T(8,128)(2,1)} %bitcast.212, bf16[4,64,1408]{2,1,0:T(8,128)(2,1)} %bitcast.209), custom_call_target="tpu_custom_call" | custom-call | flops 100000000 | bytes 2490368 | tf_op jit(solution)/shard_map/move/pallas_call | solution.py:725
  173.9 12.4 %reduce-scatter.5.cloned.1.call-start = ((), (), s32[]{:S(2)}) async-start(), calls=%async_computation.7 | async-start | bytes 6488064 | tf_op jit(solution)/shard_map/reduce_scatter | solution.py:796
  194.6 46.9 %move.12 = (f32[128,2048]{1,0:T(8,128)S(1)}, bf16[512,2048]{1,0:T(8,128)(2,1)S(1)}) custom-call(bf16[512,2048]{1,0:T(8,128)(2,1)S(1)} %convolution_convert_fusion.6.refs_0_, bf16[128,2048]{1,0:T(8,128)(2,1)S(1)} %copy-done, bf16[128,2048]{1,0:T(8,128)(2,1)S(1)} %copy.364.refs_2_), custom_call_target="tpu_custom_call" | custom-call | flops 100000000 | bytes 6291456 | tf_op jit(solution)/shard_map/move/pallas_call | solution.py:725
  244.0 33.1 %move.13 = bf16[512,2048]{1,0:T(8,128)(2,1)} custom-call(bf16[128,2048]{1,0:T(8,128)(2,1)} %multiply_convert_fusion.6.refs_0_), custom_call_target="tpu_custom_call" | custom-call | flops 100000000 | bytes 1048576 | tf_op jit(solution)/shard_map/move/pallas_call | solution.py:725
  277.2 12.6 %fusion.50 = f32[512,2816]{1,0:T(8,128)} fusion(bf16[512,2048]{1,0:T(8,128)(2,1)} %move.13, bf16[2048,2816]{1,0:T(8,128)(2,1)} %all-gather.6.cloned.1.call-done), kind=kOutput, calls=%fused_computation.134 | convolution fusion | flops 5905580032 | bytes 19398656 | tf_op jit(solution)/shard_map/dot_general | solution.py:31
  289.8 10.9 %multiply_convert_fusion.1 = (bf16[512,1408]{1,0:T(8,128)(2,1)}, bf16[512,1408]{1,0:T(8,128)(2,1)}, bf16[512,1408]{1,0:T(8,128)(2,1)S(1)}) fusion(f32[512,2816]{1,0:T(8,128)} %fusion.50, bf16[512,2048]{1,0:T(8,128)(2,1)} %copy-done.18, bf16[2048,1408]{1,0:T(8,128)(2,1)} %all-gather.8.cloned.1.call-done), kind=kOutput, calls=%fused_computation.22 | convolution fusion | flops 2963603456 | bytes 17956864 | tf_op jit(solution)/shard_map/dot_general | solution.py:31
  301.8 5.4 convolution_convert_fusion.2
  307.1 10.8 %convolution_convert_fusion.5.refs_0_ = bf16[512,2048]{1,0:T(8,128)(2,1)} fusion(bf16[2048,2816]{1,0:T(8,128)(2,1)} %all-gather.6.cloned.1.call-done, bf16[512,1408]{1,0:T(8,128)(2,1)} %get-tuple-element.164, bf16[512,1408]{1,0:T(8,128)(2,1)} %get-tuple-element.163), kind=kOutput, calls=%fused_computation.17 | convolution fusion | flops 5912395776 | bytes 16515072 | tf_op jit(solution)/shard_map/dot_general | solution.py:35
  319.6 34.8 %move.14 = f32[128,2048]{1,0:T(8,128)S(1)} custom-call(bf16[512,2048]{1,0:T(8,128)(2,1)S(1)} %copy-done.2), custom_call_target="tpu_custom_call" | custom-call | flops 100000000 | bytes 4194304 | tf_op jit(solution)/shard_map/move/pallas_call | solution.py:725
  357.2 9.1 %convolution_convert_fusion = bf16[2048,2816]{1,0:T(8,128)(2,1)} fusion(bf16[512,2048]{1,0:T(8,128)(2,1)S(1)} %copy-done.31, bf16[512,1408]{1,0:T(8,128)(2,1)S(1)} %copy-done.63, bf16[512,1408]{1,0:T(8,128)(2,1)S(1)} %copy-done.62), kind=kOutput, calls=%fused_computation | convolution fusion | flops 5917114368 | bytes 16515072 | tf_op jit(solution)/shard_map/dot_general | solution.py:39
  366.3 14.7 %reduce-scatter.5.cloned.1.call-done = bf16[256,1408]{1,0:T(8,128)(2,1)} async-done(((bf16[2048,1408]{1,0:T(8,128)(2,1)}), bf16[256,1408]{1,0:T(8,128)(2,1)}) %reduce-scatter.5.cloned.1.call-update) | async-done | bytes 720912 | tf_op jit(solution)/shard_map/reduce_scatter | solution.py:796
  381.0 6.7 %convolution_convert_fusion.7.refs_0_ = bf16[512,2048]{1,0:T(8,128)(2,1)S(1)} fusion(bf16[512,1408]{1,0:T(8,128)(2,1)} %copy-done.61, bf16[2048,1408]{1,0:T(8,128)(2,1)} %all-gather.8.cloned.1.call-done), kind=kOutput, calls=%fused_computation.19 | convolution fusion | flops 2953838592 | bytes 9306112 | tf_op jit(solution)/shard_map/dot_general | solution.py:35
  387.7 48.1 %move.15 = (f32[128,2048]{1,0:T(8,128)S(1)}, bf16[512,2048]{1,0:T(8,128)(2,1)S(1)}) custom-call(bf16[512,2048]{1,0:T(8,128)(2,1)S(1)} %convolution_convert_fusion.7.refs_0_, f32[128,2048]{1,0:T(8,128)S(1)} %get-tuple-element.57.refs_1_, bf16[128,2048]{1,0:T(8,128)(2,1)S(1)} %copy-done.1), custom_call_target="tpu_custom_call" | custom-call | flops 100000000 | bytes 6291456 | tf_op jit(solution)/shard_map/move/pallas_call | solution.py:725
  443.4 10.2 %move.16 = bf16[2,512,256]{2,1,0:T(8,128)(2,1)} custom-call(bf16[2,512,256]{2,1,0:T(8,128)(2,1)} %bitcast.217), custom_call_target="tpu_custom_call" | custom-call | flops 100000000 | bytes 1048576 | tf_op jit(solution)/shard_map/move/pallas_call | solution.py:725
  458.6 13.9 %mix_backward.1 = (bf16[1024,256]{1,0:T(8,128)(2,1)S(1)}, bf16[1024,256]{1,0:T(8,128)(2,1)S(1)}, bf16[1024,256]{1,0:T(8,128)(2,1)S(1)}, f32[1024,256]{1,0:T(8,128)}) custom-call(bf16[1024,256]{1,0:T(8,128)(2,1)S(1)} %copy-done.15, bf16[1024,256]{1,0:T(8,128)(2,1)S(1)} %copy-done.13, bf16[1024,256]{1,0:T(8,128)(2,1)S(1)} %copy-done.11, ...), custom_call_target="tpu_custom_call" | custom-call | flops 3959422976 | bytes 6291456 | tf_op jit(solution)/shard_map/mix_backward/pallas_call | solution.py:230
  484.2 50.6 %move.17 = (bf16[2,512,1024]{2,1,0:T(8,128)(2,1)}, bf16[4,64,1408]{2,1,0:T(8,128)(2,1)}, bf16[4,64,2816]{2,1,0:T(8,128)(2,1)}) custom-call(bf16[2,512,1024]{2,1,0:T(8,128)(2,1)} %bitcast.204, bf16[4,64,1408]{2,1,0:T(8,128)(2,1)} %bitcast.234, bf16[4,64,2816]{2,1,0:T(8,128)(2,1)} %bitcast.224), custom_call_target="tpu_custom_call" | custom-call | flops 100000000 | bytes 8519680 | tf_op jit(solution)/shard_map/move/pallas_call | solution.py:725
  547.7 8.3 %fusion.5 = (bf16[2048]{0:T(1024)(128)(2,1)S(1)}, bf16[512,2048]{1,0:T(8,128)(2,1)}) fusion(bf16[512,2048]{1,0:T(8,128)(2,1)S(1)} %copy-done.35, f32[512]{0:T(512)S(1)} %add_rsqrt_fusion.1, bf16[2048,1664]{1,0:T(8,128)(2,1)} %bitcast.258, bf16[512,128]{1,0:T(8,128)(2,1)S(1)} %pad.44.clone, bf16[512,512]{1,0:T(8,128)(2,1)S(1)} %copy-done.48, ...), kind=kOutput, calls=%fused_computation.11 | convolution fusion | flops 3501717504 | bytes 12720128 | tf_op jit(solution)/shard_map/dot_general | solution.py:35
  570.6 40.1 %move.18 = (f32[128,2048]{1,0:T(8,128)S(1)}, bf16[4,64,1024]{2,1,0:T(8,128)(2,1)S(1)}) custom-call(bf16[512,2048]{1,0:T(8,128)(2,1)S(1)} %copy-done.3, bf16[128,2048]{1,0:T(8,128)(2,1)S(1)} %copy-done, f32[128,2048]{1,0:T(8,128)S(1)} %get-tuple-element.162.refs_2_, f32[1,2048]{1,0:T(1,128)S(1)} %get-tuple-element.177.refs_3_, bf16[4,64,1024]{2,1,0:T(8,128)(2,1)S(1)} %bitcast.199), custom_call_target="tpu_custom_call" | custom-call | flops 100000000 | bytes 7348224 | tf_op jit(solution)/shard_map/move/pallas_call | solution.py:725
  613.4 7.4 %reduce-scatter.11.cloned.1.call-done = bf16[256,1152]{0,1:T(8,128)(2,1)} async-done(((bf16[2048,1152]{0,1:T(8,128)(2,1)}), bf16[256,1152]{0,1:T(8,128)(2,1)}) %reduce-scatter.11.cloned.1.call-update) | async-done | bytes 589840 | tf_op jit(solution)/shard_map/reduce_scatter | solution.py:796
  623.0 16.6 %move.19 = bf16[4,64,1152]{2,1,0:T(8,128)(2,1)} custom-call(bf16[4,64,1152]{2,1,0:T(8,128)(2,1)} %bitcast.210), custom_call_target="tpu_custom_call" | custom-call | flops 100000000 | bytes 1179648 | tf_op jit(solution)/shard_map/move/pallas_call | solution.py:725
  (292 shorter events, 107.8 us)
Async XLA Ops:
  7.2 183.7 %all-gather.4.cloned.1.call-start = ((), (), s32[]{:S(2)}) async-start(), calls=%async_computation.4 | async-start | bytes 2359296 | tf_op jit(solution)/shard_map/all_gather | solution.py:800
  76.6 200.6 %all-gather.6.cloned.1.call-start = ((), (), s32[]{:S(2)}) async-start(), calls=%async_computation.5 | async-start | bytes 12976128 | tf_op jit(solution)/shard_map/all_gather | solution.py:800
  78.8 399.3 %copy-start.58 = (f32[2048,1]{0,1:T(1,128)}, f32[2048,1]{0,1:T(1,128)S(1)}, u32[]{:S(2)}) copy-start(f32[2048,1]{0,1:T(1,128)S(1)} %get-tuple-element.183) | copy-start | bytes 24580
  138.1 151.6 %all-gather.8.cloned.1.call-start = ((), (), s32[]{:S(2)}) async-start(), calls=%async_computation.6 | async-start | bytes 6488064 | tf_op jit(solution)/shard_map/all_gather | solution.py:800
  142.0 11.0 %copy-start.10 = (bf16[1024,256]{1,0:T(8,128)(2,1)}, bf16[1024,256]{1,0:T(8,128)(2,1)S(1)}, u32[]{:S(2)}) copy-start(bf16[1024,256]{1,0:T(8,128)(2,1)S(1)} %get-tuple-element.170.v_ref) | copy-start | bytes 1572868
  142.0 11.0 %copy-start.12 = (bf16[1024,256]{1,0:T(8,128)(2,1)}, bf16[1024,256]{1,0:T(8,128)(2,1)S(1)}, u32[]{:S(2)}) copy-start(bf16[1024,256]{1,0:T(8,128)(2,1)S(1)} %get-tuple-element.171.k_ref) | copy-start | bytes 1572868
  142.0 11.0 %copy-start.14 = (bf16[1024,256]{1,0:T(8,128)(2,1)}, bf16[1024,256]{1,0:T(8,128)(2,1)S(1)}, u32[]{:S(2)}) copy-start(bf16[1024,256]{1,0:T(8,128)(2,1)S(1)} %get-tuple-element.172.q_ref) | copy-start | bytes 1572868
  145.2 9.1 %copy-start.41 = (bf16[64,5632]{1,0:T(8,128)(2,1)S(1)}, bf16[64,5632]{1,0:T(8,128)(2,1)}, u32[]{:S(2)}) copy-start(bf16[64,5632]{1,0:T(8,128)(2,1)} %param.39) | copy-start | bytes 2162692
  153.1 34.3 %copy-start.26 = (bf16[8,128,128]{2,1,0:T(8,128)(2,1)}, bf16[8,128,128]{2,1,0:T(8,128)(2,1)S(1)}, u32[]{:S(2)}) copy-start(bf16[8,128,128]{2,1,0:T(8,128)(2,1)S(1)} %get-tuple-element.65.score_ref) | copy-start | bytes 786436
  173.9 207.0 %reduce-scatter.5.cloned.1.call-start = ((), (), s32[]{:S(2)}) async-start(), calls=%async_computation.7 | async-start | bytes 6488064 | tf_op jit(solution)/shard_map/reduce_scatter | solution.py:796
  289.8 12.0 %copy-start.19 = (bf16[512,2048]{1,0:T(8,128)(2,1)S(1)}, bf16[512,2048]{1,0:T(8,128)(2,1)}, u32[]{:S(2)}) copy-start(bf16[512,2048]{1,0:T(8,128)(2,1)} %copy-done.18) | copy-start | bytes 6291460
  318.0 164.6 %reduce-scatter.7.cloned.1.call-start = ((), (), s32[]{:S(2)}) async-start(), calls=%async_computation.8 | async-start | bytes 12976128 | tf_op jit(solution)/shard_map/reduce_scatter | solution.py:796
  380.9 182.2 %reduce-scatter.9.cloned.1.call-start = ((), (), s32[]{:S(2)}) async-start(), calls=%async_computation.9 | async-start | bytes 4718592 | tf_op jit(solution)/shard_map/reduce_scatter | solution.py:796
  381.0 54.9 %copy-start.37 = (f32[512,1664]{1,0:T(8,128)S(1)}, f32[512,1664]{1,0:T(8,128)}, u32[]{:S(2)}) copy-start(f32[512,1664]{1,0:T(8,128)} %get-tuple-element.187) | copy-start | bytes 10223620
  387.7 48.2 %copy-start.29 = (f32[512,512]{1,0:T(8,128)S(1)}, f32[512,512]{1,0:T(8,128)}, u32[]{:S(2)}) copy-start(f32[512,512]{1,0:T(8,128)} %copy-done.28) | copy-start | bytes 3145732
  387.7 48.2 %copy-start.59 = (bf16[2048,512]{1,0:T(8,128)(2,1)S(1)}, bf16[2048,512]{1,0:T(8,128)(2,1)}, u32[]{:S(2)}) copy-start(bf16[2048,512]{1,0:T(8,128)(2,1)} %all-gather.4.cloned.1.call-done) | copy-start | bytes 6291460
  439.2 15.6 %copy-start.9 = (f32[1024,4]{1,0:T(8,128)S(1)}, f32[1024,4]{1,0:T(8,128)}, u32[]{:S(2)}) copy-start(f32[1024,4]{1,0:T(8,128)} %copy-done.8) | copy-start | bytes 49156
  439.2 15.6 %copy-start.11 = (bf16[1024,256]{1,0:T(8,128)(2,1)S(1)}, bf16[1024,256]{1,0:T(8,128)(2,1)}, u32[]{:S(2)}) copy-start(bf16[1024,256]{1,0:T(8,128)(2,1)} %copy-done.10) | copy-start | bytes 1572868
  439.2 15.6 %copy-start.13 = (bf16[1024,256]{1,0:T(8,128)(2,1)S(1)}, bf16[1024,256]{1,0:T(8,128)(2,1)}, u32[]{:S(2)}) copy-start(bf16[1024,256]{1,0:T(8,128)(2,1)} %copy-done.12) | copy-start | bytes 1572868
  458.6 13.9 %copy-start.39 = (f32[1024,256]{1,0:T(8,128)S(1)}, f32[1024,256]{1,0:T(8,128)}, u32[]{:S(2)}) copy-start(f32[1024,256]{1,0:T(8,128)} %get-tuple-element.189) | copy-start | bytes 3145732
  482.6 138.2 %reduce-scatter.11.cloned.1.call-start = ((), (), s32[]{:S(2)}) async-start(), calls=%async_computation.10 | async-start | bytes 5308416 | tf_op jit(solution)/shard_map/reduce_scatter | solution.py:796
  547.7 10.2 %copy-start.56 = (bf16[2048,1]{0,1:T(2,128)(2,1)S(1)}, bf16[2048,1]{0,1:T(2,128)(2,1)}, u32[]{:S(2)}) copy-start(bf16[2048,1]{0,1:T(2,128)(2,1)} %broadcast_in_dim.19) | copy-start | bytes 12292
  547.7 10.2 %copy-start.57 = (bf16[2048,1]{0,1:T(2,128)(2,1)S(1)}, bf16[2048,1]{0,1:T(2,128)(2,1)}, u32[]{:S(2)}) copy-start(bf16[2048,1]{0,1:T(2,128)(2,1)} %reshape.377) | copy-start | bytes 12292
  622.9 25.3 %copy-start.5 = (f32[128,2048]{1,0:T(8,128)S(1)}, f32[128,2048]{1,0:T(8,128)}, u32[]{:S(2)}) copy-start(f32[128,2048]{1,0:T(8,128)} %copy-done.4) | copy-start | bytes 3145732
  (47 other events, 125.7 us)
Sparse Core Ops, SparseCore 0:
  76.7 38.2 all-gather.3
  138.3 74.0 all-gather.5
  214.2 43.3 all-gather.7
  318.1 62.7 reduce-scatter.4
  384.7 87.7 reduce-scatter.6
  482.7 52.6 reduce-scatter.8
  564.6 56.1 reduce-scatter.10

commit v3 on v2

--- a/solution.py
+++ b/solution.py
@@ -350,14 +350,16 @@
                         self.hop(direction, step).start()
 
     def finish(self):
+        self.finish_sends()
+        self.mine.wait()
+
+    def finish_sends(self):
         for step in range(self.count - 1):
             for direction in (0, 1):
 
                 @pl.when(self.hands_on(direction, step))
                 def _():
                     self.hop(direction, step).wait_send()
-
-        self.mine.wait()
 
     @staticmethod
     def scratch(count):
@@ -437,12 +439,12 @@
     def target(self, direction, number):
         return self.count - 1 - number if direction == 0 else number
 
-    def start(self):
+    def start(self, numbers=None):
         for direction in (0, 1):
 
             @pl.when(self.me == (0 if direction == 0 else self.count - 1))
             def _():
-                for number in range(self.count - 1):
+                for number in range(self.count - 1) if numbers is None else numbers:
                     target = self.target(direction, number)
                     for piece in range(self.pieces):
                         self.hop(direction, number, piece, self.part(target, piece)).start()
@@ -738,6 +740,210 @@
     )(*values)
 
 
+LANES = 128
+TILE = 256
+
+
+def feed_forward(normed_own, mlp_piece, cotangent, number):
+    count = lax.axis_size("z")
+    own, width = normed_own.shape
+    group, ff = own * count, mlp_piece.shape[1] // 3
+    half = group // 2
+    columns = ff // LANES
+    block = width // (2 * lax.axis_size("x"))
+    per = block // TILE
+
+    def body(x_ref, w_hbm, c_hbm, sum_ref, down_ref, grad_hbm,
+             w_ref, d_ref, c_ref, normed, hidden_grad, hidden, grads, partial, stage, received,
+             load_sem, store_sem, pair_send, pair_arrive, gather_send, gather_arrive, local_sem, up, down, send, arrive):
+        me, core = lax.axis_index("z"), lax.axis_index("c")
+        loads = [
+            pltpu.make_async_copy(source, target, load_sem.at[i])
+            for i, (source, target) in enumerate(
+                [
+                    (c_hbm, c_ref),
+                    (w_hbm.at[:, pl.ds(2 * ff, ff)], d_ref),
+                    (w_hbm.at[:, pl.ds(0, 2 * ff)], w_ref),
+                ]
+            )
+        ]
+        for load in loads:
+            load.start()
+        gather = Gather("z", count, x_ref, normed, gather_send, gather_arrive, local_sem)
+        scatter = Scatter("z", count, PIECES, partial, sum_ref, up, down, send, arrive)
+        greet(line_peers("z", count) + [(True, {"c": 1 - core})])
+        gather.start()
+        loads[0].wait()
+        loads[1].wait()
+
+        def tile_of(index, size):
+            return pl.ds(pl.multiple_of(index * size, size), size)
+
+        def spans(total):
+            return [pl.ds(at, min(TILE, total - at)) for at in range(0, total, TILE)]
+
+        for at in spans(ff):
+            hidden_grad[:, at] = dot_plain(c_ref[...], d_ref[:, at])
+        loads[2].wait()
+        lower = me < count // 2
+        nearer = me // (count // 2)
+
+        def forward(rows):
+            for j in range(columns):
+                both_at, at = pl.ds(j * 2 * LANES, 2 * LANES), pl.ds(j * LANES, LANES)
+                both = dot_plain(normed[rows], w_ref[:, both_at])
+                gate, upper = both[:, :LANES], both[:, LANES:]
+                grad = hidden_grad[rows, at]
+                sig = jax.nn.sigmoid(gate)
+                silu = gate * sig
+                hidden[rows, at] = (silu * upper).astype(BF)
+                grad_gate = grad * upper * sig * (1.0 + gate * (1.0 - sig))
+                grads[rows, both_at] = jnp.concatenate(
+                    [grad_gate.astype(BF), (grad * silu).astype(BF)], axis=1
+                )
+
+        def backward(rows):
+            for at in spans(width):
+                partial[rows, at] = dot_rows(grads[rows], w_ref[at]).astype(BF)
+
+        kept = width // 2 // TILE
+
+        def rows_kept(number, by):
+            start = (number // per * 2 + by) * block + number % per * TILE
+            return pl.ds(pl.multiple_of(start, TILE), TILE)
+
+        def store(number):
+            return pltpu.make_async_copy(
+                stage.at[number % 2], grad_hbm.at[pl.ds(number * TILE, TILE)],
+                store_sem.at[number % 2],
+            )
+
+        def pass_over(number):
+            return remote(
+                stage.at[number % 2], received.at[number], pair_send.at[number % 2],
+                pair_arrive.at[number], "c", 1 - core,
+            )
+
+        def weight_rows(i):
+            ours, number = i >= kept, i % kept
+            if i >= 2:
+                if i - 2 >= kept:
+                    store(i - 2 - kept).wait()
+                else:
+                    pass_over(i - 2).wait_send()
+            at = rows_kept(number, core if ours else 1 - core)
+            slot = i % 2
+            top = dot_cols(normed[:, at], grads[...])
+            low = dot_cols(c_ref[:, at], hidden[...])
+            if ours:
+                pass_over(number).wait_recv()
+                top = top + received[number, :, : 2 * ff].astype(F32)
+                low = low + received[number, :, 2 * ff :].astype(F32)
+            stage[slot, :, : 2 * ff] = top.astype(BF)
+            stage[slot, :, 2 * ff :] = low.astype(BF)
+            if ours:
+                store(number).start()
+            else:
+                pass_over(number).start()
+            at = pl.ds(i * TILE, TILE)
+            down_ref[:, at] = dot_rows(hidden[...], d_ref[at]).astype(BF)
+
+        def away(near):
+            block = jnp.where(lower, count // 2, count // 2 - 1)
+            end = jnp.where(lower, count - 1, 0)
+            return tile_of(block if near else end, own)
+
+        gather.run(1)
+        gather.mine.wait()
+        forward(tile_of(nearer, half))
+        gather.run(2)
+        forward(away(True))
+        gather.run(3)
+        forward(away(False))
+        backward(away(False))
+        scatter.start([0])
+        backward(away(True))
+        scatter.start([1])
+        backward(tile_of(nearer, half))
+        scatter.start([2])
+        units = list(range(width // TILE))
+        stages = [(step, far) for step in range(count - 1) for far in (False, True)]
+        spare = len(units) - len(stages)
+        for i in units[: max(spare, 0)]:
+            weight_rows(i)
+        rest = units[max(spare, 0) :]
+        for step, far in stages:
+            scatter.run(step, far)
+            if rest:
+                weight_rows(rest.pop(0))
+        scatter.finish()
+        gather.finish_sends()
+        for number in range(kept - 2, kept):
+            store(number).wait()
+
+    in_vmem, anywhere = pl.BlockSpec(memory_space=pltpu.VMEM), pl.BlockSpec(memory_space=pl.ANY)
+    return pl.pallas_call(
+        body,
+        in_specs=[in_vmem, anywhere, anywhere],
+        out_specs=[in_vmem, in_vmem, anywhere],
+        out_shape=[
+            jax.ShapeDtypeStruct((own, width), F32),
+            jax.ShapeDtypeStruct((group, width), BF),
+            jax.ShapeDtypeStruct((width // 2, 3 * ff), BF),
+        ],
+        scratch_shapes=[
+            pltpu.VMEM((width, 2 * ff), BF),
+            pltpu.VMEM((width, ff), BF),
+            pltpu.VMEM((group, width), BF),
+            pltpu.VMEM((group, width), BF),
+            pltpu.VMEM((group, ff), F32),
+            pltpu.VMEM((group, ff), BF),
+            pltpu.VMEM((group, 2 * ff), BF),
+            pltpu.VMEM((group, width), BF),
+            pltpu.VMEM((2, TILE, 3 * ff), BF),
+            pltpu.VMEM((width // 2 // TILE, TILE, 3 * ff), BF),
+            pltpu.SemaphoreType.DMA((3,)),
+            pltpu.SemaphoreType.DMA((2,)),
+            pltpu.SemaphoreType.DMA((2,)),
+            pltpu.SemaphoreType.DMA((width // 2 // TILE,)),
+        ]
+        + Gather.scratch(count)
+        + Scatter.scratch(count, own, width, PIECES),
+        compiler_params=pltpu.CompilerParams(
+            collective_id=number, has_side_effects=True, vmem_limit_bytes=60 * 1024 * 1024
+        ),
+        cost_estimate=pl.CostEstimate(
+            flops=WAIT_FLOPS, bytes_accessed=width * ff * 12, transcendentals=0
+        ),
+        name="feed_forward",
+    )(normed_own, mlp_piece, cotangent)
+
+
+def join(values, parts):
+    Z, rows = values[0].shape[:2]
+
+    def body(*refs):
+        ins, outs = refs[: len(values)], refs[len(values) :]
+        for out_ref, (index, start, size, turns, turn) in zip(outs, parts):
+            held = ins[index]
+            if turns == 1:
+                out_ref[...] = held[0, :, start : start + size].astype(F32)
+            else:
+                for j in range(size // LANES):
+                    at = start + (j * turns + turn) * LANES
+                    out_ref[:, j * LANES : (j + 1) * LANES] = held[0, :, at : at + LANES].astype(F32)
+
+    return pl.pallas_call(
+        body,
+        grid=(Z,),
+        in_specs=[pl.BlockSpec((1,) + v.shape[1:], lambda i: (i, 0, 0)) for v in values],
+        out_specs=[pl.BlockSpec((rows, part[2]), lambda i: (0, i)) for part in parts],
+        out_shape=[jax.ShapeDtypeStruct((rows, Z * part[2]), F32) for part in parts],
+        compiler_params=pltpu.CompilerParams(dimension_semantics=("arbitrary",)),
+        name="join",
+    )(*values)
+
+
 def local(
     tokens, doc_lengths, cotangent, attn_gain, query_weight, key_weight, value_weight, gate_weight,
     rank_in, rank_out, decay_bias, head_gain, out_weight, mlp_gain, mlp_gate_weight,
@@ -778,9 +984,6 @@
     def swap_y(value):
         return move(next(numbers), swaps=[(value, "y")])[0]
 
-    def gather_z(value):
-        return move(next(numbers), gathers=[(value, "z")])[0]
-
     def after(value, *others):
         return lax.optimization_barrier((value,) + others)[0]
 
@@ -792,8 +995,8 @@
         cut = value.reshape(Z, Y, own, value.shape[-1])
         return jnp.swapaxes(cut, 0, 1).reshape(Y, group, value.shape[-1])
 
-    def scatter_rest(value):
-        sums = lax.psum_scatter(value, REST, scatter_dimension=0, tiled=True)
+    def scatter_rest(value, axes=REST):
+        sums = lax.psum_scatter(value, axes, scatter_dimension=0, tiled=True)
         return sums.reshape(Z, rows, -1)
 
     def gather_rest(value):
@@ -817,10 +1020,14 @@
         first, own_tokens, cut_columns(out_weight), (X, C, Z, Y), next(numbers)
     )
     input_weights = input_weights.reshape(width, -1)
-    mlp_weights = jnp.concatenate(
-        [cut_columns(mlp_gate_weight), cut_columns(mlp_up_weight)], axis=2
-    )
-    down_weights = cut_columns(down_weight)
+    mlp_weights = jnp.stack(
+        [
+            cut_columns(w).reshape(Z, rows, ff // LANES, LANES)
+            for w in (mlp_gate_weight, mlp_up_weight)
+        ],
+        axis=3,
+    ).reshape(Z, rows, 2 * ff)
+    mlp_weights = jnp.concatenate([mlp_weights, cut_columns(down_weight)], axis=2)
 
     projected = 2 * DK + 2 * DV
     near = 2 * DK + DV
@@ -871,10 +1078,7 @@
     seg_rows = cut.astype(F32)[:, None, :]
 
     mixed_part, enter, scores = mix_forward(queries, keys, value_part, log_decay, aux, seg_rows)
-    mixed_part, down_weights = move(
-        next(numbers), swaps=[(from_sequence(mixed_part), "y"), (down_weights, "z")]
-    )
-    down_piece = gather_rest(down_weights)
+    mixed_part = swap_y(from_sequence(mixed_part))
     mixed = jnp.swapaxes(mixed_part, 0, 1).reshape(group, DV).astype(F32)
 
     head_scale = lax.rsqrt(jnp.mean(mixed * mixed, axis=1, keepdims=True) + head_eps)
@@ -891,36 +1095,18 @@
     )
     scale_mid = lax.rsqrt(jnp.mean(residual * residual, axis=1, keepdims=True) + norm_eps)
     hat_mid = residual * scale_mid
-    normed_mlp = gather_z((hat_mid * mlp_gain_all).astype(BF))
-
-    both_pre = dot_plain(normed_mlp, mlp_piece)
-    gate_pre = both_pre[:, :ff]
-    up_pre = both_pre[:, ff:]
-    sig_gate = jax.nn.sigmoid(gate_pre)
-    silu_gate = gate_pre * sig_gate
-    hidden = (silu_gate * up_pre).astype(BF)
-    grad_hidden = dot_plain(group_cotangent, down_piece)
-    grad_gate = (grad_hidden * up_pre * sig_gate * (1.0 + gate_pre * (1.0 - sig_gate))).astype(BF)
-    grad_up = (grad_hidden * silu_gate).astype(BF)
-    grad_both = jnp.concatenate([grad_gate, grad_up], axis=1)
-    out_partial = dot_rows(hidden, down_piece).astype(BF)
-    mlp_back, down_partial = lax.optimization_barrier(
-        (
-            dot_rows(grad_both, mlp_piece).astype(BF),
-            dot_cols(group_cotangent, hidden).astype(BF),
-        )
-    )
-    down_sums = scatter_rest(down_partial)
-    grad_normed_mlp = move(next(numbers), scatter=(mlp_back, "z"))[0]
-    mlp_partial = dot_cols(normed_mlp, grad_both).astype(BF)
+    normed_mlp = (hat_mid * mlp_gain_all).astype(BF)
+    grad_normed_mlp, out_partial, mlp_partial = feed_forward(
+        normed_mlp, mlp_piece, group_cotangent, next(numbers)
+    )
+    mlp_sums = scatter_rest(mlp_partial, ("x", "y"))
 
     mlp_gain_part = jnp.sum(grad_normed_mlp * hat_mid, axis=0)
     scaled = grad_normed_mlp * mlp_gain_all
     grad_residual = own_cotangent.astype(F32) + scale_mid * (
         scaled - hat_mid * jnp.mean(scaled * hat_mid, axis=1, keepdims=True)
     )
-    branch_own, mlp_partial = lax.optimization_barrier((grad_residual.astype(BF), mlp_partial))
-    mlp_sums = scatter_rest(after(mlp_partial, down_sums))
+    branch_own = grad_residual.astype(BF)
     layer_out, grad_branch = move(
         next(numbers), scatter=(out_partial, "z"), gathers=[(branch_own, "z")],
         extras=[residual], post=lambda total_sum, rest: straight(total_sum + rest),
@@ -945,10 +1131,8 @@
         [dot_cols(normed_in, grad_out_gate), dot_cols(grad_branch, gated)], axis=1
     ).astype(BF)
     back, side_partial = lax.optimization_barrier((back, side_partial))
-    side_sums = scatter_rest(after(side_partial, mlp_sums))
-    back, down_rows, mlp_rows = move(
-        next(numbers), swaps=[(back, "y"), (down_sums, "z"), (mlp_sums, "z")]
-    )
+    side_sums = scatter_rest(side_partial)
+    back, mlp_rows = move(next(numbers), swaps=[(back, "y"), (mlp_sums, "z")])
     summed = jnp.sum(back[:, :, : 3 * DK].astype(F32), axis=0).astype(BF)
     grad_value = jnp.swapaxes(back[:, :, 3 * DK :], 0, 1).reshape(group, DV)
     grad_logit = summed[:, 2 * DK :]
@@ -995,7 +1179,7 @@
     partial, near_partial = lax.optimization_barrier(
         (normed_in_partial.astype(BF), near_partial)
     )
-    near_sums = scatter_rest(after(near_partial, side_sums))
+    near_sums = scatter_rest(near_partial)
 
     def finish_tokens(back_sum, x, grad_res, gain):
         held = x.astype(F32)
@@ -1011,27 +1195,32 @@
     )
     near_rows = move(next(numbers), swaps=[(after(near_sums, tokens_grad), "z")])[0]
 
-    def joined(value):
-        return jnp.swapaxes(value, 0, 1).reshape(rows, -1).astype(F32)
-
+    mlp_grads = join(
+        [mlp_rows], [(0, 0, ff, 2, 0), (0, 0, ff, 2, 1), (0, 2 * ff, ff, 1, 0)]
+    )
+    query_grad, key_grad, value_grad, gate_grad, out_grad = join(
+        [near_rows, side_rows],
+        [
+            (0, 0, DK, 1, 0), (0, DK, DK, 1, 0), (0, 2 * DK, DV, 1, 0),
+            (1, 0, DV, 1, 0), (1, DV, DV, 1, 0),
+        ],
+    )
     small_rows = jnp.sum(near_rows[:, :, near : near + SMALL].astype(F32), axis=0)
     return (
         layer_out,
         tokens_grad,
         small_rows[:, R],
-        joined(near_rows[:, :, :DK]),
-        joined(near_rows[:, :, DK : 2 * DK]),
-        joined(near_rows[:, :, 2 * DK : near]),
-        joined(side_rows[:, :, :DV]),
+        query_grad,
+        key_grad,
+        value_grad,
+        gate_grad,
         small_rows[:, :R],
         small_rows[: rows * H * DK // width, R + 2 : 2 * R + 2],
         small_rows[: rows * H * DK // width, 2 * R + 2],
         small_rows[: rows * DV // width, 2 * R + 3],
-        joined(side_rows[:, :, DV:]),
+        out_grad,
         small_rows[:, R + 1],
-        joined(mlp_rows[:, :, :ff]),
-        joined(mlp_rows[:, :, ff:]),
-        joined(down_rows),
+        *mlp_grads,
     )
 
 

time: 659 us -> 615 us (0.933); the launches traced: 657 us -> 607 us
  matrix products: 89.1 us -> 35 us
  Pallas kernels: 427 us -> 445 us
  starting transfers between devices: 12.8 us -> 0.63 us
  local copies, waits for them, and re-layouts: 64.9 us -> 58 us
    pallas_call x0 -> x3, Pallas kernels: none -> 92.4 us  [the longest x1 84.7 us: feed_forward(): pl.pallas_call(body, in_specs=[in_vmem, anywhere, anywhere], out_specs=[i...]
    pallas_call x10 -> x8, Pallas kernels: 345 us -> 270 us  [move(): pl.pallas_call(body, in_specs=in_specs, out_specs=out_specs, out_shape=sh...]
    dot_general x5 -> x3, matrix products: 34.6 us -> 11.1 us  [dot_plain(): return jnp.dot(left, right, preferred_element_type=F32)]
    dot_general x5 -> x3, matrix products: 31.7 us -> 15.4 us  [dot_rows(): lax.dot_general(left, right, (((1,), (1,)), ((), ())), preferred_element_...]
    dot_general x6 -> x4, matrix products: 22.7 us -> 8.55 us  [dot_cols(): lax.dot_general(left, right, (((0,), (0,)), ((), ())), preferred_element_...]
    reduce_scatter x4 -> x3, starting transfers between devices: 12.7 us -> 0.55 us  [scatter_rest(): sums = lax.psum_scatter(value, axes, scatter_dimension=0, tiled=True)]
    all_gather x3 -> x2, waiting for transfers between devices: 0.04 us -> 10.9 us  [gather_rest(): return lax.all_gather(value.reshape(Z * rows, -1), REST, axis=0, tiled=True)]
    convert_element_type x8 -> x0, local copies, waits for them, and re-layouts: 7.63 us -> none  [joined(): return jnp.swapaxes(value, 0, 1).reshape(rows, -1).astype(F32)]
  transfers between devices with their start and end apart: 7 -> 5, of which waited for: 2 -> 2; matrix products, arithmetic and copies ran while one was open for 17% -> 15% of each run, Pallas kernels for 53% -> 46%
where the time goes in v3:
time: 615 us; the launch traced here: 607 us
  Pallas kernels  445 us (72%)
  local copies, waits for them, and re-layouts  58 us (9%)
  matrix products  35 us (6%)
  waiting for transfers between devices  28.6 us (5%)
  other arithmetic  24.1 us (4%)
  between operations  15.4 us (3%)
    pallas_call x8, Pallas kernels, move(): pl.pallas_call(body, in_specs=in_specs, out_specs=out_specs, out_shape=sh...  270 us
    pallas_call x1, Pallas kernels, feed_forward(): pl.pallas_call(body, in_specs=[in_vmem, anywhere, anywhere], out_specs=[i...  84.7 us
    pallas_call x1, Pallas kernels, spread_and_gather(): pl.pallas_call(body, in_specs=[anywhere] * 3, out_specs=[anywhere] * 3, o...  60.5 us
    unnamed x139, local copies, waits for them, and re-layouts  22.2 us
    reduce_scatter x3, waiting for transfers between devices, scatter_rest(): sums = lax.psum_scatter(value, axes, scatter_dimension=0, tiled=True)  17.6 us
    dot_general x3, matrix products, dot_rows(): lax.dot_general(left, right, (((1,), (1,)), ((), ())), preferred_element_...  15.4 us
    pallas_call x1, Pallas kernels, mix_backward(): pl.pallas_call(mix_backward_body, grid=(count,), in_specs=[tokens(DK), to...  13.7 us
  transfers between devices with their start and end apart: 5, of which 2 were waited for; matrix products, arithmetic and copies ran while one was open for 15% of the time, Pallas kernels for 46%

profile of v3, /device:TPU:9, one launch (start us, length us, event | category | flops | bytes accessed | tf_op | source)
XLA Modules:
  0.0 606.6 jit_solution(8509801654606499448)
XLA Ops:
  12.1 60.5 %spread_and_gather.1 = (bf16[32,64,1664]{2,1,0:T(8,128)(2,1)}, bf16[512,2048]{1,0:T(8,128)(2,1)}, bf16[4,64,512]{2,1,0:T(8,128)(2,1)}) custom-call(bf16[4,64,1664]{2,1,0:T(8,128)(2,1)} %copy-done.38, bf16[128,2048]{1,0:T(8,128)(2,1)} %copy.312.x_ref.refs_1_, bf16[4,64,512]{2,1,0:T(8,128)(2,1)} %bitcast.187), custom_call_target="tpu_custom_call" | custom-call | flops 100000000 | bytes 6815744 | tf_op jit(solution)/shard_map/spread_and_gather/pallas_call | solution.py:635
  74.8 8.7 %fusion.46 = (bf16[512,1664]{1,0:T(8,128)(2,1)S(1)}, f32[512,1664]{1,0:T(8,128)}) fusion(bf16[2048,1664]{1,0:T(8,128)(2,1)} %bitcast.209, bf16[512,2048]{1,0:T(8,128)(2,1)S(1)} %copy-done.35, f32[2048]{0:T(1024)S(1)} %bitcast.216, f32[512]{0:T(512)S(1)} %add_rsqrt_fusion.1), kind=kOutput, calls=%fused_computation.114 | convolution fusion | flops 3494707200 | bytes 14034944 | tf_op jit(solution)/shard_map/dot_general | solution.py:31
  97.0 54.9 %move.8 = (bf16[2,512,896]{2,1,0:T(8,128)(2,1)}, bf16[4,64,4224]{2,1,0:T(8,128)(2,1)}) custom-call(bf16[2,512,896]{2,1,0:T(8,128)(2,1)} %pad_maximum_fusion.4.refs_0_, bf16[4,64,4224]{2,1,0:T(8,128)(2,1)} %pad_maximum_fusion.1.refs_1_), custom_call_target="tpu_custom_call" | custom-call | flops 100000000 | bytes 7995392 | tf_op jit(solution)/shard_map/move/pallas_call | solution.py:727
  156.0 3.1 fusion.22
  159.1 7.9 %mix_forward.1 = (bf16[1024,256]{1,0:T(8,128)(2,1)S(1)}, bf16[8,256,256]{2,1,0:T(8,128)(2,1)S(1)}, bf16[8,128,128]{2,1,0:T(8,128)(2,1)S(1)}) custom-call(bf16[1024,256]{1,0:T(8,128)(2,1)S(1)} %get-tuple-element.171.q_ref, bf16[1024,256]{1,0:T(8,128)(2,1)S(1)} %get-tuple-element.170.k_ref, bf16[1024,256]{1,0:T(8,128)(2,1)S(1)} %get-tuple-element.169.v_ref, ...), custom_call_target="tpu_custom_call" | custom-call | flops 2080374784 | bytes 4194304 | tf_op jit(solution)/shard_map/mix_forward/pallas_call | solution.py:200
  168.2 13.8 %move.9 = bf16[2,512,256]{2,1,0:T(8,128)(2,1)} custom-call(bf16[2,512,256]{2,1,0:T(8,128)(2,1)} %bitcast.178), custom_call_target="tpu_custom_call" | custom-call | flops 100000000 | bytes 1048576 | tf_op jit(solution)/shard_map/move/pallas_call | solution.py:727
  187.6 3.1 convolution_convert_fusion.3.refs_0_
  190.7 46.4 %move.10 = (f32[128,2048]{1,0:T(8,128)S(1)}, bf16[512,2048]{1,0:T(8,128)(2,1)S(1)}) custom-call(bf16[512,2048]{1,0:T(8,128)(2,1)S(1)} %convolution_convert_fusion.3.refs_0_, bf16[128,2048]{1,0:T(8,128)(2,1)S(1)} %copy-done, bf16[128,2048]{1,0:T(8,128)(2,1)S(1)} %copy.332.refs_2_), custom_call_target="tpu_custom_call" | custom-call | flops 100000000 | bytes 6291456 | tf_op jit(solution)/shard_map/move/pallas_call | solution.py:727
  239.6 10.9 %all-gather.5.cloned.1.call-done.w_hbm = bf16[2048,4224]{1,0:T(8,128)(2,1)} async-done(((bf16[256,4224]{1,0:T(8,128)(2,1)}), bf16[2048,4224]{1,0:T(8,128)(2,1)}) %all-gather.5.cloned.1.call-update) | async-done | bytes 17301520 | tf_op jit(solution)/shard_map/all_gather | solution.py:1003
  250.5 84.7 %feed_forward.1 = (f32[128,2048]{1,0:T(8,128)}, bf16[512,2048]{1,0:T(8,128)(2,1)}, bf16[1024,4224]{1,0:T(8,128)(2,1)}) custom-call(bf16[128,2048]{1,0:T(8,128)(2,1)} %multiply_convert_fusion.3.x_ref, bf16[2048,4224]{1,0:T(8,128)(2,1)} %all-gather.5.cloned.1.call-done.w_hbm, bf16[512,2048]{1,0:T(8,128)(2,1)} %copy-done.1), custom_call_target="tpu_custom_call" | custom-call | flops 100000000 | bytes 34603008 | tf_op jit(solution)/shard_map/feed_forward/pallas_call | solution.py:885
  338.5 44.5 %move.11 = (f32[128,2048]{1,0:T(8,128)S(1)}, bf16[512,2048]{1,0:T(8,128)(2,1)S(1)}) custom-call(bf16[512,2048]{1,0:T(8,128)(2,1)S(1)} %copy-done.2, f32[128,2048]{1,0:T(8,128)S(1)} %get-tuple-element.57.refs_1_, bf16[128,2048]{1,0:T(8,128)(2,1)S(1)} %get-tuple-element.163.refs_2_), custom_call_target="tpu_custom_call" | custom-call | flops 100000000 | bytes 6291456 | tf_op jit(solution)/shard_map/move/pallas_call | solution.py:727
  390.7 9.5 %move.12 = bf16[2,512,256]{2,1,0:T(8,128)(2,1)} custom-call(bf16[2,512,256]{2,1,0:T(8,128)(2,1)} %bitcast.181), custom_call_target="tpu_custom_call" | custom-call | flops 100000000 | bytes 1048576 | tf_op jit(solution)/shard_map/move/pallas_call | solution.py:727
  405.1 13.7 %mix_backward.1 = (bf16[1024,256]{1,0:T(8,128)(2,1)S(1)}, bf16[1024,256]{1,0:T(8,128)(2,1)S(1)}, bf16[1024,256]{1,0:T(8,128)(2,1)S(1)}, f32[1024,256]{1,0:T(8,128)}) custom-call(bf16[1024,256]{1,0:T(8,128)(2,1)S(1)} %copy-done.16, bf16[1024,256]{1,0:T(8,128)(2,1)S(1)} %copy-done.14, bf16[1024,256]{1,0:T(8,128)(2,1)S(1)} %copy-done.12, ...), custom_call_target="tpu_custom_call" | custom-call | flops 3959422976 | bytes 6291456 | tf_op jit(solution)/shard_map/mix_backward/pallas_call | solution.py:230
  426.3 2.6 pad_maximum_fusion
  429.4 50.5 %move.13 = (bf16[2,512,1024]{2,1,0:T(8,128)(2,1)}, bf16[4,64,4224]{2,1,0:T(8,128)(2,1)}) custom-call(bf16[2,512,1024]{2,1,0:T(8,128)(2,1)} %bitcast.164, bf16[4,64,4224]{2,1,0:T(8,128)(2,1)} %bitcast.174), custom_call_target="tpu_custom_call" | custom-call | flops 100000000 | bytes 8519680 | tf_op jit(solution)/shard_map/move/pallas_call | solution.py:727
  485.8 4.7 convolution_convert_fusion
  490.4 2.6 slice.156
  495.4 9.2 %fusion.5 = (bf16[2048]{0:T(1024)(128)(2,1)S(1)}, bf16[512,2048]{1,0:T(8,128)(2,1)}) fusion(bf16[512,2048]{1,0:T(8,128)(2,1)} %get-tuple-element.52, f32[512]{0:T(512)S(1)} %copy-done.54, bf16[2048,1664]{1,0:T(8,128)(2,1)} %bitcast.210, bf16[512,128]{1,0:T(8,128)(2,1)S(1)} %pad.44.clone, bf16[512,512]{1,0:T(8,128)(2,1)S(1)} %copy-done.42, ...), kind=kOutput, calls=%fused_computation.9 | convolution fusion | flops 3501717504 | bytes 12720128 | tf_op jit(solution)/shard_map/dot_general | solution.py:35
  505.3 5.0 fusion.3
  513.2 34.3 %move.14 = (f32[128,2048]{1,0:T(8,128)S(1)}, bf16[4,64,1024]{2,1,0:T(8,128)(2,1)S(1)}) custom-call(bf16[512,2048]{1,0:T(8,128)(2,1)S(1)} %copy-done.3, bf16[128,2048]{1,0:T(8,128)(2,1)S(1)} %copy-done, f32[128,2048]{1,0:T(8,128)S(1)} %get-tuple-element.164.refs_2_, f32[1,2048]{1,0:T(1,128)S(1)} %get-tuple-element.174.refs_3_, bf16[4,64,1024]{2,1,0:T(8,128)(2,1)S(1)} %bitcast.159), custom_call_target="tpu_custom_call" | custom-call | flops 100000000 | bytes 7348224 | tf_op jit(solution)/shard_map/move/pallas_call | solution.py:727
  549.2 4.2 join.3
  553.4 17.6 %reduce-scatter.8.cloned.1.call-done = bf16[256,1152]{0,1:T(8,128)(2,1)} async-done(((bf16[2048,1152]{0,1:T(8,128)(2,1)}), bf16[256,1152]{0,1:T(8,128)(2,1)}) %reduce-scatter.8.cloned.1.call-update) | async-done | bytes 589840 | tf_op jit(solution)/shard_map/reduce_scatter | solution.py:999
  573.1 16.6 %move.15.refs_0_ = bf16[4,64,1152]{2,1,0:T(8,128)(2,1)} custom-call(bf16[4,64,1152]{2,1,0:T(8,128)(2,1)} %bitcast.172), custom_call_target="tpu_custom_call" | custom-call | flops 100000000 | bytes 1179648 | tf_op jit(solution)/shard_map/move/pallas_call | solution.py:727
  592.7 3.6 join.2
  (269 shorter events, 79.0 us)
Async XLA Ops:
  7.3 3.8 copy-start.49
  7.3 3.8 copy-start.46
  7.3 3.8 copy-start.47
  7.3 180.3 %all-gather.3.cloned.1.call-start = ((), (), s32[]{:S(2)}) async-start(), calls=%async_computation.3 | async-start | bytes 2359296 | tf_op jit(solution)/shard_map/all_gather | solution.py:1003
  72.6 177.9 %all-gather.5.cloned.1.call-start = ((), (), s32[]{:S(2)}) async-start(), calls=%async_computation.4 | async-start | bytes 19464192 | tf_op jit(solution)/shard_map/all_gather | solution.py:1003
  74.8 8.7 %copy-start.53 = (f32[512]{0:T(512)}, f32[512]{0:T(512)S(1)}, u32[]{:S(2)}) copy-start(f32[512]{0:T(512)S(1)} %add_rsqrt_fusion.1) | copy-start | bytes 6148
  151.9 277.5 %reduce-scatter.4.cloned.1.call-start = ((), (), s32[]{:S(2)}) async-start(), calls=%async_computation.5 | async-start | bytes 10813440 | tf_op jit(solution)/shard_map/reduce_scatter | solution.py:999
  155.9 11.0 %copy-start.11 = (bf16[1024,256]{1,0:T(8,128)(2,1)}, bf16[1024,256]{1,0:T(8,128)(2,1)S(1)}, u32[]{:S(2)}) copy-start(bf16[1024,256]{1,0:T(8,128)(2,1)S(1)} %get-tuple-element.169.v_ref) | copy-start | bytes 1572868
  156.0 11.0 %copy-start.13 = (bf16[1024,256]{1,0:T(8,128)(2,1)}, bf16[1024,256]{1,0:T(8,128)(2,1)S(1)}, u32[]{:S(2)}) copy-start(bf16[1024,256]{1,0:T(8,128)(2,1)S(1)} %get-tuple-element.170.k_ref) | copy-start | bytes 1572868
  156.0 11.0 %copy-start.15 = (bf16[1024,256]{1,0:T(8,128)(2,1)}, bf16[1024,256]{1,0:T(8,128)(2,1)S(1)}, u32[]{:S(2)}) copy-start(bf16[1024,256]{1,0:T(8,128)(2,1)S(1)} %get-tuple-element.171.q_ref) | copy-start | bytes 1572868
  159.1 7.9 %copy-start.23 = (f32[1024,256]{1,0:T(8,128)}, f32[1024,256]{1,0:T(8,128)S(1)}, u32[]{:S(2)}) copy-start(f32[1024,256]{1,0:T(8,128)S(1)} %get-tuple-element.181.ld_ref) | copy-start | bytes 3145732
  167.0 16.4 %copy-start.25 = (bf16[8,128,128]{2,1,0:T(8,128)(2,1)}, bf16[8,128,128]{2,1,0:T(8,128)(2,1)S(1)}, u32[]{:S(2)}) copy-start(bf16[8,128,128]{2,1,0:T(8,128)(2,1)S(1)} %get-tuple-element.64.score_ref) | copy-start | bytes 786436
  335.2 175.1 %reduce-scatter.6.cloned.1.call-start = ((), (), s32[]{:S(2)}) async-start(), calls=%async_computation.6 | async-start | bytes 4718592 | tf_op jit(solution)/shard_map/reduce_scatter | solution.py:999
  336.4 46.7 %copy-start.57 = (bf16[2048,512]{1,0:T(8,128)(2,1)S(1)}, bf16[2048,512]{1,0:T(8,128)(2,1)}, u32[]{:S(2)}) copy-start(bf16[2048,512]{1,0:T(8,128)(2,1)} %all-gather.3.cloned.1.call-done) | copy-start | bytes 6291460
  336.8 46.3 %copy-start.37 = (f32[512,1664]{1,0:T(8,128)S(1)}, f32[512,1664]{1,0:T(8,128)}, u32[]{:S(2)}) copy-start(f32[512,1664]{1,0:T(8,128)} %get-tuple-element.180) | copy-start | bytes 10223620
  337.1 46.0 %copy-start.28 = (f32[512,512]{1,0:T(8,128)S(1)}, f32[512,512]{1,0:T(8,128)}, u32[]{:S(2)}) copy-start(f32[512,512]{1,0:T(8,128)} %copy-done.27) | copy-start | bytes 3145732
  386.4 14.8 %copy-start.9 = (f32[1024,4]{1,0:T(8,128)S(1)}, f32[1024,4]{1,0:T(8,128)}, u32[]{:S(2)}) copy-start(f32[1024,4]{1,0:T(8,128)} %copy-done.8) | copy-start | bytes 49156
  386.4 14.8 %copy-start.12 = (bf16[1024,256]{1,0:T(8,128)(2,1)S(1)}, bf16[1024,256]{1,0:T(8,128)(2,1)}, u32[]{:S(2)}) copy-start(bf16[1024,256]{1,0:T(8,128)(2,1)} %copy-done.11) | copy-start | bytes 1572868
  386.4 14.8 %copy-start.14 = (bf16[1024,256]{1,0:T(8,128)(2,1)S(1)}, bf16[1024,256]{1,0:T(8,128)(2,1)}, u32[]{:S(2)}) copy-start(bf16[1024,256]{1,0:T(8,128)(2,1)} %copy-done.13) | copy-start | bytes 1572868
  405.1 13.7 %copy-start.39 = (f32[1024,256]{1,0:T(8,128)S(1)}, f32[1024,256]{1,0:T(8,128)}, u32[]{:S(2)}) copy-start(f32[1024,256]{1,0:T(8,128)} %get-tuple-element.182) | copy-start | bytes 3145732
  428.9 142.1 %reduce-scatter.8.cloned.1.call-start = ((), (), s32[]{:S(2)}) async-start(), calls=%async_computation.7 | async-start | bytes 5308416 | tf_op jit(solution)/shard_map/reduce_scatter | solution.py:999
  495.4 9.5 %slice-start = ((bf16[2048,1152]{0,1:T(8,128)(2,1)}), bf16[2048,16]{0,1:T(8,128)(2,1)S(1)}, s32[]{:S(2)}) async-start(bf16[2048,1152]{0,1:T(8,128)(2,1)} %copy-done.33), calls=%async_computation.8 | async-start | bytes 131072 | tf_op jit(solution)/shard_map/slice | solution.py:1168
  553.4 44.3 %copy-start.5 = (f32[128,2048]{1,0:T(8,128)S(1)}, f32[128,2048]{1,0:T(8,128)}, u32[]{:S(2)}) copy-start(f32[128,2048]{1,0:T(8,128)} %copy-done.4) | copy-start | bytes 3145732
  573.1 25.5 %copy-start.7 = (f32[128,2048]{1,0:T(8,128)S(1)}, f32[128,2048]{1,0:T(8,128)}, u32[]{:S(2)}) copy-start(f32[128,2048]{1,0:T(8,128)} %copy-done.6) | copy-start | bytes 3145732
  (43 other events, 87.9 us)
Sparse Core Ops, SparseCore 0:
  72.7 32.6 all-gather.2
  152.0 98.3 all-gather.4
  335.3 91.9 reduce-scatter.3
  430.6 56.0 reduce-scatter.5
  510.4 60.4 reduce-scatter.7
